TPU v7x, 32 devices: a whole 2x2x4 slice. The times are simulated.
32 devices in a mesh: member: 2 (over y), lat: 8 (over z, core), lon: 2 (over x), lev: 1.
Axes of the slice: x: 2, y: 2, z: 4, core: 2. Of those that a mesh axis runs over, the one named last changes fastest.
Arguments:
- adjoint: float32 [6, 32, 64, 3072], P('member', 'lev', 'lat', 'lon'), parts along dimension 0, may hold values from -6 to 6
- depth: bfloat16 [32, 64, 3072], P('lev', 'lat', 'lon'), may hold values from 0.5 to 2
- zonal_coef: float32 [64], replicated, may hold values from 0.05 to 0.5
- merid_coef: float32 [64], replicated, may hold values from 0.05 to 0.5
- coriolis: float32 [64], replicated, may hold values from -0.5 to 0.5
- layer_weight: float32 [32], P('lev'), may hold values from 0.02 to 0.2
- cutoffs: int32 [64], replicated, may hold values from 0 to 1023, as said below
- polar_flags: int32 [64], replicated, may hold values from 0 to 1, as said below
Outputs:
- adjoint_next: float32 [6, 32, 64, 3072], P('member', 'lev', 'lat', 'lon'), parts along dimension 0
There are 2 independent parts, one for each index of `member`. A program takes and returns all parts, laid end to end along the dimension named above; an argument that names none is the same for every part. Nothing has to cross between parts.
Inputs may be any that keep to these rules, and one draw needn't show every extreme that they name: cutoffs[0] is 1023 and cutoffs[63] is 0. `polar_flags`: the flagged rows form one run that starts at row 0 and one that ends at row 63; each run has 12 to 24 rows, and one of the two has exactly 24.
All inputs are finite; a program needn't handle non-finite values.
Results may differ from a plain program's by a relative error of at most 0.0003.
Values sent between devices are 32-bit elements; how exact they have to be, the bound alone decides.
A program may use at most 128 MiB of HBM per device.

v0:
```python
import functools
import math

import jax
import jax.numpy as jnp
import ml_dtypes
import numpy as np
from jax import lax
from jax.experimental import pallas as pl
from jax.experimental.pallas import tpu as pltpu
from jax.sharding import PartitionSpec as P

KMAX = 1024
POLE_ROWS = 24


def extended(cells, sides, width, closed):
    for axis, dim in sides:
        count = lax.axis_size(axis)
        ends = count if closed else count - 1
        head = lax.slice_in_dim(cells, 0, width, axis=dim)
        tail = lax.slice_in_dim(cells, cells.shape[dim] - width, cells.shape[dim], axis=dim)
        cells = jnp.concatenate(
            [
                lax.ppermute(tail, axis, [(i, (i + 1) % count) for i in range(ends)]),
                cells,
                lax.ppermute(head, axis, [((i + 1) % count, i) for i in range(ends)]),
            ],
            axis=dim,
        )
    return cells


def entering(value, axis, join, neutral):
    count, mine = (lax.axis_size(axis), lax.axis_index(axis))
    pieces = lax.all_gather(value, axis)
    total = jnp.full_like(value, 0) + jnp.asarray(neutral, value.dtype)

    def turn(position, total):
        longer = join(total, pieces[position])
        return jnp.where(position < mine, longer, total)

    return lax.fori_loop(0, count - 1, turn, total)


def wave_table(col_count, wave_start, wave_count, circle):
    columns = lax.iota(jnp.int32, col_count)
    wave_index = wave_start + lax.iota(jnp.int32, wave_count)
    phase = columns[:, None] * wave_index[None, :] % circle
    angle = phase.astype(jnp.float32) * (2.0 * math.pi / circle)
    return jnp.concatenate([jnp.cos(angle), jnp.sin(angle)], axis=1)


def keep_weights(cut_rows, wave_start, wave_count, circle):
    wave_index = wave_start + lax.iota(jnp.int32, wave_count)
    factor = jnp.where(wave_index == 0, 1.0, 2.0) / circle
    kept = (wave_index[None, :] <= cut_rows[:, None]).astype(jnp.float32) * factor[None, :]
    return jnp.concatenate([kept, kept], axis=1)


def block_width():
    return min(KMAX, 128)


def project_rows(row_data, cut_rows):
    circle = row_data.shape[1]
    width = block_width()
    result = jnp.zeros(row_data.shape, jnp.float32)
    for block_index in range(KMAX // width):
        table = wave_table(circle, block_index * width, width, circle)
        coefs = jnp.dot(
            row_data, table, precision=lax.Precision.HIGHEST, preferred_element_type=jnp.float32
        )
        weights = keep_weights(cut_rows, block_index * width, width, circle)
        result = result + jnp.dot(
            coefs * weights,
            table.T,
            precision=lax.Precision.HIGHEST,
            preferred_element_type=jnp.float32,
        )
    return result


def transpose_filter(row_data, cut_rows, flag_rows):
    lon_count = lax.axis_size("lon")
    lon_index = lax.axis_index("lon")
    share = row_data.shape[0] // lon_count
    full_rows = lax.all_to_all(row_data, "lon", split_axis=0, concat_axis=1, tiled=True)
    my_cuts = lax.dynamic_slice_in_dim(cut_rows, lon_index * share, share)
    smoothed = project_rows(full_rows, my_cuts)
    returned = lax.all_to_all(smoothed, "lon", split_axis=1, concat_axis=0, tiled=True)
    return jnp.where(flag_rows[:, None] > 0, returned, row_data)


def polar_filter(row_data, cut_rows, flag_rows):
    return transpose_filter(row_data, cut_rows, flag_rows)


def on_device(adjoint, depth, zonal_coef, merid_coef, coriolis, layer_weight, cutoffs, polar_flags):
    fields, level_count, lat_rows, lon_cells = adjoint.shape
    lat_index = lax.axis_index("lat")
    lat_total = lat_rows * lax.axis_size("lat")
    stacked = adjoint.reshape(fields * level_count, lat_rows, lon_cells)
    bands = lax.all_to_all(stacked, "lat", split_axis=0, concat_axis=1, tiled=True)
    groups = bands.shape[0]
    polar_block = jnp.concatenate([bands[:, :POLE_ROWS], bands[:, lat_total - POLE_ROWS :]], axis=1)
    polar_cuts = jnp.concatenate([cutoffs[:POLE_ROWS], cutoffs[lat_total - POLE_ROWS :]])
    polar_marks = jnp.concatenate([polar_flags[:POLE_ROWS], polar_flags[lat_total - POLE_ROWS :]])
    row_data = polar_block.reshape(groups * 2 * POLE_ROWS, lon_cells)
    cut_rows = jnp.tile(polar_cuts, groups)
    flag_rows = jnp.tile(polar_marks, groups)
    treated = polar_filter(row_data, cut_rows, flag_rows)
    treated = treated.reshape(groups, 2 * POLE_ROWS, lon_cells)
    bands = jnp.concatenate(
        [
            treated[:, :POLE_ROWS],
            bands[:, POLE_ROWS : lat_total - POLE_ROWS],
            treated[:, POLE_ROWS:],
        ],
        axis=1,
    )
    filtered = lax.all_to_all(bands, "lat", split_axis=1, concat_axis=0, tiled=True).reshape(
        adjoint.shape
    )
    q_height = filtered[0]
    q_east = filtered[1]
    q_north = filtered[2]
    zonal_rows = lax.dynamic_slice_in_dim(zonal_coef, lat_index * lat_rows, lat_rows)[None, :, None]
    merid_rows = lax.dynamic_slice_in_dim(merid_coef, lat_index * lat_rows, lat_rows)[None, :, None]
    coriolis_rows = lax.dynamic_slice_in_dim(coriolis, lat_index * lat_rows, lat_rows)[
        None, :, None
    ]
    height_flux = depth.astype(jnp.float32) * q_height
    north_pair = jnp.stack([merid_rows * q_north, merid_rows * height_flux])
    north_rims = extended(north_pair, (("lat", 2),), 1, False)
    merid_diff = north_rims[:, :, :-2] - north_rims[:, :, 2:]
    east_pair = jnp.stack([q_east, height_flux])
    east_rims = extended(east_pair, (("lon", 3),), 1, True)
    zonal_diff = zonal_rows * (east_rims[..., :-2] - east_rims[..., 2:])
    column_force = -zonal_diff[0] - merid_diff[0]
    running = jnp.cumsum(column_force, axis=0)
    carried = entering(
        jnp.sum(column_force, axis=0), "lev", jnp.add, jnp.zeros((lat_rows, lon_cells), jnp.float32)
    )
    new_height = adjoint[0] + layer_weight[:, None, None] * (running + carried[None])
    new_east = adjoint[1] - zonal_diff[1] - coriolis_rows * q_north
    new_north = adjoint[2] - merid_diff[1] + coriolis_rows * q_east
    return jnp.stack([new_height, new_east, new_north])


RANK = 60
TILE = 256
LANES = 128


def halves(value):
    high = value.astype(jnp.bfloat16)
    return high, (value - high.astype(jnp.float32)).astype(jnp.bfloat16)


def split_table(value):
    high = np.asarray(value, np.float32).astype(ml_dtypes.bfloat16)
    low = (np.asarray(value, np.float32) - high.astype(np.float32)).astype(ml_dtypes.bfloat16)
    return high, low


@functools.lru_cache(maxsize=None)
def kernel_tables(cells):
    circle = 2 * cells

    def kernel(distance):
        wave = circle * np.sin(np.pi * (distance % (2 * circle)) / circle)
        return np.where(distance % circle == 0, 0.0, 1.0 / np.where(distance % circle == 0, 1.0, wave))

    n = np.arange(cells)
    rest = kernel(n[:, None] - n[None, :] - cells)
    columns, rows = [], []
    for _ in range(RANK):
        i, j = divmod(int(np.argmax(np.abs(rest))), cells)
        pivot = rest[i, j]
        size = np.sqrt(abs(pivot))
        u, v = rest[:, j] / pivot * size, rest[i, :] / size
        columns.append(u)
        rows.append(v)
        rest = rest - u[:, None] * v[None, :]
    project = np.stack(
        rows
        + [kernel(cells - 1 - n), kernel(0 - n), kernel(cells - 1 - n - cells), kernel(0 - n - cells)],
        axis=1,
    )
    expand = np.zeros((64, cells))
    expand[:RANK] = np.stack(columns)
    band = kernel(np.arange(2 * cells)[None, :] - np.arange(LANES)[:, None] - cells)
    return project, expand, band.astype(np.float32)


def project_kernel(x_ref, trig_ref, mix_ref, edge_ref, depth_ref, table_ref, out_ref):
    x = x_ref[...]
    fields, levels, rows, cells = x.shape
    cos, sin = trig_ref[0][None, None], trig_ref[1][None, None]

    def spectrum(value):
        high, low = halves(value.reshape(fields * levels * rows, cells))
        total = jnp.dot(high, table_ref[...], preferred_element_type=jnp.float32)
        total = total + jnp.dot(low, table_ref[...], preferred_element_type=jnp.float32)
        total = total + pltpu.roll(total, 64, 1)
        return total.reshape(fields, levels, rows, LANES)

    z = mix_ref[0][None, None] * spectrum(x * cos) + mix_ref[1][None, None] * spectrum(x * sin)
    lane = lax.broadcasted_iota(jnp.int32, (1, 1, rows, LANES), 3)
    z = z + jnp.where(lane == RANK, edge_ref[0][None, None] * x[..., cells - 1 :], 0.0)
    z = z + jnp.where(lane == RANK + 1, edge_ref[0][None, None] * x[..., :1], 0.0)
    depth = depth_ref[...].astype(jnp.float32)
    z = z + jnp.where(lane == 124, depth[None, :, :, cells - 1 :], 0.0)
    z = z + jnp.where(lane == 125, depth[None, :, :, :1], 0.0)
    out_ref[...] = z


def local_row(row, x_ref, trig_ref, coef_ref, band_ref, terms_ref, band_high, band_low, total_ref):
    cells = trig_ref.shape[2] // 2
    lines = cells // LANES * 8
    count = x_ref.shape[0] // lines
    blocks = cells // TILE
    chosen = lax.broadcasted_iota(jnp.int32, (8, LANES), 0) == row

    def line(values):
        return jnp.sum(jnp.where(chosen, values, 0.0), axis=0, keepdims=True)

    def strip(block):
        return pl.ds(block * 8 + row, count, stride=lines)

    coef = line(coef_ref[...])
    keep = coef[:, 3:4]
    for block in range(blocks):
        x = jnp.concatenate([x_ref[strip(2 * block), :], x_ref[strip(2 * block + 1), :]], axis=1)
        high, low = halves(x)
        at = pl.ds(block * count, count)
        terms_ref[at, :] = jnp.concatenate([high, low, high], axis=1)
        total_ref[at, :] = keep * x

    def upright(which):
        values = coef[:, 4:5] * line(trig_ref[which, :, cells : cells + LANES])
        return jnp.broadcast_to(values, (LANES, LANES)).T

    inner_cos, inner_sin = upright(0), upright(1)
    def build(block):
        at = pl.ds(block * LANES, LANES)
        value = band_ref[:, at] * (line(trig_ref[1, :, at]) * inner_cos - line(trig_ref[0, :, at]) * inner_sin)
        high, low = halves(value)
        band_high[:, at] = high
        band_low[:, at] = low

    def multiply(shift):
        first = cells + TILE * shift
        weights = jnp.concatenate(
            [
                table[:, from_ : from_ + TILE]
                for table in (band_high, band_high, band_low)
                for from_ in (first, first - LANES)
            ],
            axis=0,
        )
        start, stop = max(0, -shift), min(blocks, blocks - shift)
        source = pl.ds(start * count, (stop - start) * count)
        target = pl.ds((start + shift) * count, (stop - start) * count)
        value = jnp.dot(terms_ref[source, :], weights, preferred_element_type=jnp.float32)
        total_ref[target, :] += value

    builds = [functools.partial(build, block) for block in range(2 * cells // LANES)]
    return builds, [functools.partial(multiply, shift) for shift in range(1 - blocks, blocks)]


def local_pair(rows, *refs):
    arrays, scratch = refs[:4], refs[4:]
    builds, products = local_row(rows[0], *arrays, *scratch[:4])
    for build in builds:
        build()
    later_builds, later_products = local_row(rows[1], *arrays, *scratch[4:])
    for turn, product in enumerate(products):
        product()
        for build in later_builds[turn :: len(products)]:
            build()
    for product in later_products:
        product()


def rim_kernel(x_ref, trig_ref, coef_ref, band_ref, y_ref, *scratch):
    local_pair((0, 7), x_ref, trig_ref, coef_ref, band_ref, *scratch)
    count = y_ref.shape[1]
    for turn in range(2):
        for block in range(y_ref.shape[2] // TILE):
            y_ref[turn, :, pl.ds(block * TILE, TILE)] = scratch[4 * turn + 3][pl.ds(block * count, count), :]


def inner_kernel(x_ref, trig_ref, coef_ref, band_ref, rim_ref, sent_ref, ends_ref, y_ref, *scratch):
    del sent_ref, ends_ref
    step = pl.program_id(0)
    _, count, cells = rim_ref.shape
    lines = cells // LANES * 8

    @pl.when(step < 3)
    def _():
        local_pair((2 * step + 1, 2 * step + 2), x_ref, trig_ref, coef_ref, band_ref, *scratch)
        for turn in range(2):
            for block in range(cells // LANES):
                part = pl.ds(block // 2 * count, count)
                value = scratch[4 * turn + 3][part, pl.ds(block % 2 * LANES, LANES)]
                y_ref[pl.ds(block * 8 + 2 * step + 1 + turn, count, stride=lines), :] = value

    @pl.when(step == 3)
    def _():
        for turn in range(2):
            for block in range(cells // LANES):
                value = rim_ref[turn, :, pl.ds(block * LANES, LANES)]
                y_ref[pl.ds(block * 8 + 7 * turn, count, stride=lines), :] = value


def expanded(z, table_ref):
    turned = pltpu.roll(z, 64, 1)
    first = lax.broadcasted_iota(jnp.int32, z.shape, 1) < 64
    results = []
    for twice in (jnp.where(first, z, turned), jnp.where(first, turned, z)):
        terms = jnp.concatenate(halves(twice), axis=1)
        results.append(jnp.dot(terms, table_ref[...], preferred_element_type=jnp.float32))
    return results


def border_kernel(z_ref, y_ref, trig_ref, coef_ref, depth_ref, expand_ref, first_ref, last_ref):
    _, count, cells = y_ref.shape
    levels = depth_ref.shape[0]
    depth = depth_ref[...].astype(jnp.float32)
    for turn, row, ref in ((0, 0, first_ref), (1, 7, last_ref)):
        z = z_ref[pl.ds(row, count, stride=8), :]
        with_cos, with_sin = expanded(z, expand_ref)
        q = y_ref[turn] + trig_ref[0, row : row + 1] * with_cos + trig_ref[1, row : row + 1] * with_sin
        merid = coef_ref[row : row + 1, 1:2]
        ref[0] = merid * q[2 * levels :]
        ref[1] = merid * (depth[:, row, :] * q[:levels])


def final_kernel(
    weight_ref, x_ref, y_ref, z_ref, trig_ref, coef_ref, depth_ref, expand_ref, before_ref, after_ref, rims_ref,
    out_ref, q_ref, run_ref,
):
    step = pl.program_id(0)
    fields, levels, rows, cells = x_ref.shape
    coef = coef_ref[...]
    zonal, merid, coriolis = coef[:, 0:1], coef[:, 1:2], coef[:, 2:3]
    row = lax.broadcasted_iota(jnp.int32, (rows, cells), 0)
    column = lax.broadcasted_iota(jnp.int32, (rows, cells), 1)

    z = z_ref[...].reshape(fields * levels * rows, LANES)
    q = y_ref[...]
    for turn, value in enumerate(expanded(z, expand_ref)):
        q = q + trig_ref[turn][None, None] * value.reshape(fields, levels, rows, cells)
    q_ref[...] = q

    def zonal_adjoint(value, west, east):
        left = jnp.where(column == 0, west, pltpu.roll(value, 1, 1))
        right = jnp.where(column == cells - 1, east, pltpu.roll(value, cells - 1, 1))
        return zonal * (left - right)

    def merid_adjoint(value, before, after):
        value = merid * value
        up = jnp.where(row == 0, before, pltpu.roll(value, 1, 0))
        down = jnp.where(row == rows - 1, after, pltpu.roll(value, rows - 1, 0))
        return up - down

    @pl.when(step == 0)
    def _():
        run_ref[...] = jnp.zeros_like(run_ref)

    for level in range(levels):
        height, east, north = q_ref[0, level], q_ref[1, level], q_ref[2, level]
        flux = depth_ref[level].astype(jnp.float32) * height
        rims = rims_ref[level]
        line = pl.ds(level, 1)
        run_ref[...] -= zonal_adjoint(east, rims[:, 0:1], rims[:, 1:2]) + merid_adjoint(
            north, before_ref[0, line, :], after_ref[0, line, :]
        )
        out_ref[0, level] = x_ref[0, level] + weight_ref[step * levels + level] * run_ref[...]
        out_ref[1, level] = x_ref[1, level] - zonal_adjoint(flux, rims[:, 2:3], rims[:, 3:4]) - coriolis * north
        out_ref[2, level] = (
            x_ref[2, level]
            - merid_adjoint(flux, before_ref[1, line, :], after_ref[1, line, :])
            + coriolis * east
        )


def whole(array):
    shape = array.shape
    return pl.BlockSpec(shape, lambda *_: (0,) * len(shape))


def on_pair(adjoint, depth, zonal_coef, merid_coef, coriolis, layer_weight, cutoffs, polar_flags):
    fields, level_count, rows, cells = adjoint.shape
    circle = 2 * cells
    lat_count = lax.axis_size("lat")
    first_row = lax.axis_index("lat") * rows
    project, expand, band = kernel_tables(cells)
    project_high, project_low = split_table(project)
    project_table = jnp.asarray(np.concatenate([project_high, project_low], axis=1))
    expand_high, expand_low = split_table(expand)
    expand_table = jnp.asarray(
        np.concatenate([expand_high, expand_low, expand_high, np.zeros_like(expand_high)])
    )

    def mine(values):
        return lax.dynamic_slice_in_dim(values, first_row, rows)

    cuts, flags = mine(cutoffs), mine(polar_flags)
    kept = 2 * cuts + 1
    offsets = lax.iota(jnp.int32, circle) - cells
    phase = (kept[:, None] * offsets[None, :]) % (2 * circle)
    angle = phase.astype(jnp.float32) * (math.pi / circle)
    cos, sin = jnp.cos(angle), jnp.sin(angle)
    on = (flags > 0).astype(jnp.float32)[:, None]
    keep = jnp.where(flags > 0, kept.astype(jnp.float32) / circle, 1.0)[:, None]
    sign = on * jnp.where(cuts % 2 == 0, -1.0, 1.0)[:, None]
    own_cos, own_sin = cos[:, cells:], sin[:, cells:]
    trig = jnp.stack([own_cos, own_sin])
    cross = jnp.stack([sign * own_cos, sign * own_sin])
    around = jnp.stack([cos, sin])
    one, zero = jnp.ones((rows, RANK), jnp.float32), jnp.zeros((rows, RANK), jnp.float32)
    blank = jnp.zeros((rows, 4), jnp.float32)
    end_cos, end_sin = own_cos[:, cells - 1 :], own_sin[:, cells - 1 :]
    start_cos, start_sin = own_cos[:, :1], own_sin[:, :1]
    mix = jnp.stack(
        [
            jnp.concatenate(
                [one, on * end_sin, on * start_sin, sign * end_cos, sign * start_cos, zero, blank], axis=1
            ),
            jnp.concatenate(
                [zero, -on * end_cos, -on * start_cos, sign * end_sin, sign * start_sin, one, blank], axis=1
            ),
        ]
    )
    coef = jnp.concatenate(
        [
            mine(zonal_coef)[:, None],
            mine(merid_coef)[:, None],
            mine(coriolis)[:, None],
            keep,
            on,
            jnp.zeros((rows, LANES - 5), jnp.float32),
        ],
        axis=1,
    )
    edge = keep[None]

    part = 8
    steps = level_count // part
    four = pl.BlockSpec((fields, part, rows, cells), lambda i: (0, i, 0, 0))
    three = pl.BlockSpec((part, rows, cells), lambda i: (i, 0, 0))
    code = pl.BlockSpec((fields, part, rows, LANES), lambda i: (0, i, 0, 0))
    lines = pl.BlockSpec((2, part, cells), lambda i: (0, i, 0))
    limit = pltpu.CompilerParams(vmem_limit_bytes=48 * 2**20)
    count = fields * level_count * rows

    z = pl.pallas_call(
        project_kernel,
        grid=(steps,),
        in_specs=[four, whole(trig), whole(mix), whole(edge), three, whole(project_table)],
        out_specs=code,
        out_shape=jax.ShapeDtypeStruct((fields, level_count, rows, LANES), jnp.float32),
        compiler_params=limit,
    )(adjoint, trig, mix, edge, depth, project_table)
    arrived = lax.ppermute(z, "lon", [(0, 1), (1, 0)])

    circles = fields * level_count
    tiles = (circles, rows, cells // LANES, LANES)
    flat = adjoint.reshape(tiles).transpose(0, 2, 1, 3).reshape(-1, LANES)
    strip = circles * cells // TILE
    scratch = [
        pltpu.VMEM((strip, 3 * TILE), jnp.bfloat16),
        pltpu.VMEM((LANES, circle), jnp.bfloat16),
        pltpu.VMEM((LANES, circle), jnp.bfloat16),
        pltpu.VMEM((strip, TILE), jnp.float32),
    ]
    band = jnp.asarray(band)

    def cost(done):
        return pl.CostEstimate(
            flops=6 * done * circles * cells * cells, bytes_accessed=8 * count * cells, transcendentals=0
        )

    rim = pl.pallas_call(
        rim_kernel,
        grid=(1,),
        in_specs=[whole(flat), whole(around), whole(coef), whole(band)],
        out_specs=pl.BlockSpec((2, circles, cells), lambda i: (0, 0, 0)),
        out_shape=jax.ShapeDtypeStruct((2, circles, cells), jnp.float32),
        scratch_shapes=2 * scratch,
        cost_estimate=cost(2),
        compiler_params=limit,
    )(flat, around, coef, band)

    sent = arrived.reshape(count, LANES)
    edges = jax.ShapeDtypeStruct((2, level_count, cells), jnp.float32)
    first, last = pl.pallas_call(
        border_kernel,
        grid=(1,),
        in_specs=[whole(sent), whole(rim), whole(cross), whole(coef), whole(depth), whole(expand_table)],
        out_specs=[whole(edges), whole(edges)],
        out_shape=[edges, edges],
        compiler_params=limit,
    )(sent, rim, cross, coef, depth, expand_table)
    before = lax.ppermute(last, "lat", [(i, i + 1) for i in range(lat_count - 1)])
    after = lax.ppermute(first, "lat", [(i + 1, i) for i in range(lat_count - 1)])

    rims = arrived[:2, ..., RANK : RANK + 2] + z[:2, ..., RANK + 2 : RANK + 4]
    rims = jnp.concatenate([rims[1], rims[0] * arrived[0, ..., 124:126]], axis=-1)

    y = pl.pallas_call(
        inner_kernel,
        grid=(rows // 2,),
        in_specs=[
            whole(flat),
            whole(around),
            whole(coef),
            whole(band),
            whole(rim),
            pl.BlockSpec(memory_space=pl.ANY),
            pl.BlockSpec(memory_space=pl.ANY),
        ],
        out_specs=whole(flat),
        out_shape=jax.ShapeDtypeStruct(flat.shape, jnp.float32),
        scratch_shapes=2 * scratch,
        cost_estimate=cost(rows - 2),
        compiler_params=limit,
    )(flat, around, coef, band, rim, first, rims)
    y = y.reshape(tiles[0], tiles[2], rows, LANES).transpose(0, 2, 1, 3).reshape(adjoint.shape)

    return pl.pallas_call(
        final_kernel,
        grid=(steps,),
        in_specs=[
            pl.BlockSpec(memory_space=pltpu.SMEM),
            four,
            four,
            code,
            whole(cross),
            whole(coef),
            three,
            whole(expand_table),
            lines,
            lines,
            pl.BlockSpec((part, rows, 4), lambda i: (i, 0, 0)),
        ],
        out_specs=four,
        out_shape=jax.ShapeDtypeStruct(adjoint.shape, jnp.float32),
        scratch_shapes=[
            pltpu.VMEM((fields, part, rows, cells), jnp.float32),
            pltpu.VMEM((rows, cells), jnp.float32),
        ],
        compiler_params=limit,
    )(layer_weight, adjoint, y, arrived, cross, coef, depth, expand_table, before, after, rims)


def plan_for(mesh):
    return on_pair if mesh.shape["lon"] == 2 and mesh.shape["lev"] == 1 else on_device


def solution(mesh):
    return jax.shard_map(
        plan_for(mesh),
        mesh=mesh,
        in_specs=(
            P("member", "lev", "lat", "lon"),
            P("lev", "lat", "lon"),
            P(),
            P(),
            P(),
            P("lev"),
            P(),
            P(),
        ),
        out_specs=P("member", "lev", "lat", "lon"),
        check_vma=False,
    )
```

profile of v0, /device:TPU:1, one launch (start us, length us, event | category | flops | bytes accessed | tf_op | source)
XLA Modules:
  0.0 56.9 jit_solution(15765781687931091444)
XLA Ops:
  0.0 0.0 copy-start
  0.0 0.0 copy-start.7
  0.0 0.8 %fusion.17 = (f32[1,8,1]{1,2,0:T(1,128)S(1)}, pred[8]{0:T(512)(128)(4,1)S(1)}, s32[8]{0:T(128)S(1)}) fusion(s32[64]{0:T(128)} %param.18, s32[]{:T(128)S(6)} %select_n.41, s32[64]{0:T(128)} %param.17), kind=kLoop, calls=%fused_computation.54 | loop fusion | flops 48 | bytes 140 | tf_op jit(solution)/shard_map/broadcast_in_dim;broadcast_in_dim | solution.py:449
  0.8 0.7 %fusion.15 = (f32[8]{0:T(128)S(1)}, f32[8,1]{0,1:T(1,128)S(1)}, f32[8,1]{0,1:T(1,128)S(1)}) fusion(pred[8]{0:T(512)(128)(4,1)S(1)} %get-tuple-element.10, s32[64]{0:T(128)} %param.17, s32[]{:T(128)S(6)} %select_n.41, s32[8]{0:T(128)S(1)} %get-tuple-element.11), kind=kLoop, calls=%fused_computation.44 | loop fusion | flops 152 | bytes 172 | tf_op jit(solution)/shard_map/mul | solution.py:419
  1.5 0.1 copy.48
  1.6 0.1 copy.53
  1.7 0.1 copy.57.edge_ref
  1.8 0.1 copy.51
  1.9 0.5 fusion.8
  2.3 0.1 multiply_bitcast_fusion.1
  2.4 0.1 slice_multiply_fusion.6
  2.5 0.1 concatenate.13
  2.6 0.1 concatenate.14
  2.7 0.0 copy-start.1
  2.7 1.1 %copy-done.1 = bf16[32,8,1536]{2,1,0:T(8,128)(2,1)S(1)} copy-done((bf16[32,8,1536]{2,1,0:T(8,128)(2,1)S(1)}, bf16[32,8,1536]{2,1,0:T(8,128)(2,1)}, u32[]{:S(2)}) %copy-start.1) | copy-done | bytes 786456
  3.8 1.0 %copy-done.4 = bf16[1536,128]{1,0:T(8,128)(2,1)S(1)} copy-done((bf16[1536,128]{1,0:T(8,128)(2,1)S(1)}, bf16[1536,128]{1,0:T(8,128)(2,1)}, u32[]{:S(2)}) %copy-start.4) | copy-done | bytes 393240
  4.8 5.7 %shard_map.110 = f32[3,32,8,128]{3,2,1,0:T(8,128)S(1)} custom-call(f32[3,32,8,1536]{3,2,1,0:T(8,128)} %x_ref.3, f32[2,8,1536]{2,1,0:T(8,128)S(1)} %pad_maximum_fusion.2.trig_ref, f32[2,8,128]{2,1,0:T(8,128)S(1)} %pad_maximum_fusion.4.mix_ref, f32[1,8,1]{2,1,0:T(8,128)S(1)} %copy.57.edge_ref, bf16[32,8,1536]{2,1,0:T(8,128)(2,1)S(1)} %copy-done.1, ...), custom_call_target="tpu_custom_call" | custom-call | tf_op jit(solution)/shard_map/pallas_call | solution.py:460
  10.5 2.1 %collective-permute-start = (f32[3,32,8,128]{3,2,1,0:T(8,128)S(1)}, f32[3,32,8,128]{3,2,1,0:T(8,128)S(1)}, u32[]{:S(2)}, u32[]{:S(2)}) collective-permute-start(f32[3,32,8,128]{3,2,1,0:T(8,128)S(1)} %shard_map.110), channel_id=1, source_target_pairs={{0,1},{1,0},{2,3},{3,2},{4,5},{5,4},{6,7},{7,6},{8,9},{9,8},{10,11... | collective-permute-start | bytes 1179656 | tf_op jit(solution)/shard_map/ppermute | solution.py:468
  12.6 0.5 fusion.12
  13.1 0.0 copy-done
  13.1 0.1 dynamic-slice_bitcast_fusion.2
  13.2 0.0 copy-done.7
  13.2 0.0 copy-done.8
  13.2 0.1 dynamic-slice_bitcast_fusion
  13.3 0.1 copy.46
  13.3 0.1 copy.44
  13.4 0.1 copy.47
  13.5 0.1 copy.45
  13.6 0.1 concatenate.12.coef_ref
  13.7 0.0 copy-done.6
  13.7 0.0 copy-start.2
  13.7 0.0 copy-start.3
  13.7 6.3 %shard_map.109.y_ref.rim_ref = f32[2,96,1536]{2,1,0:T(8,128)S(1)} custom-call(f32[9216,128]{1,0:T(8,128)} %bitcast.41, f32[2,8,3072]{2,1,0:T(8,128)S(1)} %pad_maximum_fusion.trig_ref, f32[8,128]{1,0:T(8,128)S(1)} %concatenate.12.coef_ref, f32[128,3072]{1,0:T(8,128)S(1)} %copy-done.6), custom_call_target="tpu_custom_call" | custom-call | flops 2717908992 | bytes 9437184 | tf_op jit(solution)/shard_map/pallas_call | solution.py:487
  20.1 1.4 %collective-permute-done.z_ref = f32[3,32,8,128]{3,2,1,0:T(8,128)S(1)} collective-permute-done((f32[3,32,8,128]{3,2,1,0:T(8,128)S(1)}, f32[3,32,8,128]{3,2,1,0:T(8,128)S(1)}, u32[]{:S(2)}, u32[]{:S(2)}) %collective-permute-start) | collective-permute-done | bytes 393248 | tf_op jit(solution)/shard_map/ppermute | solution.py:468
  21.4 0.0 copy-done.2
  21.4 0.0 copy-done.3
  21.4 0.8 %shard_map.111 = (f32[2,32,1536]{2,1,0:T(8,128)S(1)}, f32[2,32,1536]{2,1,0:T(8,128)S(1)}) custom-call(f32[768,128]{1,0:T(8,128)S(1)} %bitcast.40, f32[2,96,1536]{2,1,0:T(8,128)S(1)} %shard_map.109.y_ref.rim_ref, f32[2,8,1536]{2,1,0:T(8,128)S(1)} %pad_maximum_fusion.3.trig_ref, f32[8,128]{1,0:T(8,128)S(1)} %concatenate.12.coef_ref, ...), custom_call_target="tpu_custom_call" | custom-call | tf_op jit(solution)/shard_map/pallas_call | solution.py:500
  22.3 4.6 %collective-permute-start.1 = (f32[2,32,1536]{2,1,0:T(8,128)S(1)}, f32[2,32,1536]{2,1,0:T(8,128)S(1)}, u32[]{:S(2)}, u32[]{:S(2)}) collective-permute-start(f32[2,32,1536]{2,1,0:T(8,128)S(1)} %get-tuple-element.8), channel_id=1, source_target_pairs={{0,2},{2,4},{4,6},{6,8},{8,10},{10,12},{12,14},{1,3},{3,5},{5,7},{... | collective-permute-start | bytes 1179656 | tf_op jit(solution)/shard_map/ppermute | solution.py:508
  26.9 2.1 %collective-permute-start.2 = (f32[2,32,1536]{2,1,0:T(8,128)S(1)}, f32[2,32,1536]{2,1,0:T(8,128)S(1)}, u32[]{:S(2)}, u32[]{:S(2)}) collective-permute-start(f32[2,32,1536]{2,1,0:T(8,128)S(1)} %get-tuple-element.7.sent_ref), channel_id=1, source_target_pairs={{2,0},{4,2},{6,4},{8,6},{10,8},{12,10},{14,12},{3,1},{5,3},{7,5},{... | collective-permute-start | bytes 1179656 | tf_op jit(solution)/shard_map/ppermute | solution.py:509
  29.0 0.2 slice_add_fusion
  29.2 0.1 slice_bitcast_fusion
  29.3 0.1 pad_maximum_fusion.1.ends_ref.rims_ref
  29.4 0.0 copy-start.5
  29.4 18.9 %shard_map.112 = f32[9216,128]{1,0:T(8,128)} custom-call(f32[9216,128]{1,0:T(8,128)} %bitcast.42, f32[2,8,3072]{2,1,0:T(8,128)S(1)} %pad_maximum_fusion.trig_ref, f32[8,128]{1,0:T(8,128)S(1)} %concatenate.12.coef_ref, f32[128,3072]{1,0:T(8,128)S(1)} %copy-done.6, f32[2,96,1536]{2,1,0:T(8,128)S(1)} %shard_map.109.y_ref.rim_ref, ...), custom_call_target="tpu_custom_call" | custom-call | flops 8153726976 | bytes 9437184 | tf_op jit(solution)/shard_map/pallas_call | solution.py:514
  48.3 0.0 collective-permute-done.1.before_ref
  48.3 0.0 collective-permute-done.2.after_ref
  48.3 0.0 copy-done.5
  48.3 8.5 %shard_map.113 = f32[3,32,8,1536]{3,2,1,0:T(8,128)} custom-call(f32[32]{0:T(128)S(1)} %copy-done.5, f32[3,32,8,1536]{3,2,1,0:T(8,128)} %x_ref.3, f32[3,32,8,1536]{3,2,1,0:T(8,128)} %bitcast.43, f32[3,32,8,128]{3,2,1,0:T(8,128)S(1)} %collective-permute-done.z_ref, f32[2,8,1536]{2,1,0:T(8,128)S(1)} %pad_maximum_fusion.3.trig_ref, ...), custom_call_target="tpu_custom_call" | custom-call | tf_op jit(solution)/shard_map/pallas_call | solution.py:534
  (13 shorter events, 0.1 us)
Async XLA Ops:
  0.0 13.1 %copy-start = (f32[64]{0:T(128)S(1)}, f32[64]{0:T(128)}, u32[]{:S(2)}) copy-start(f32[64]{0:T(128)} %param.13) | copy-start | bytes 772
  0.0 13.2 %copy-start.7 = (f32[64]{0:T(128)S(1)}, f32[64]{0:T(128)}, u32[]{:S(2)}) copy-start(f32[64]{0:T(128)} %param.15) | copy-start | bytes 772
  0.0 13.2 %copy-start.8 = (f32[64]{0:T(128)S(1)}, f32[64]{0:T(128)}, u32[]{:S(2)}) copy-start(f32[64]{0:T(128)} %param.14) | copy-start | bytes 772
  2.7 1.1 %copy-start.1 = (bf16[32,8,1536]{2,1,0:T(8,128)(2,1)S(1)}, bf16[32,8,1536]{2,1,0:T(8,128)(2,1)}, u32[]{:S(2)}) copy-start(bf16[32,8,1536]{2,1,0:T(8,128)(2,1)} %depth_ref.5) | copy-start | bytes 2359300
  3.8 1.0 %copy-start.4 = (bf16[1536,128]{1,0:T(8,128)(2,1)S(1)}, bf16[1536,128]{1,0:T(8,128)(2,1)}, u32[]{:S(2)}) copy-start(bf16[1536,128]{1,0:T(8,128)(2,1)} %constant.64.clone.table_ref) | copy-start | bytes 1179652
  4.8 8.9 %copy-start.6 = (f32[128,3072]{1,0:T(8,128)S(1)}, f32[128,3072]{1,0:T(8,128)}, u32[]{:S(2)}) copy-start(f32[128,3072]{1,0:T(8,128)} %constant.66.clone.band_ref) | copy-start | bytes 4718596
  10.5 10.9 %collective-permute-start = (f32[3,32,8,128]{3,2,1,0:T(8,128)S(1)}, f32[3,32,8,128]{3,2,1,0:T(8,128)S(1)}, u32[]{:S(2)}, u32[]{:S(2)}) collective-permute-start(f32[3,32,8,128]{3,2,1,0:T(8,128)S(1)} %shard_map.110), channel_id=1, source_target_pairs={{0,1},{1,0},{2,3},{3,2},{4,5},{5,4},{6,7},{7,6},{8,9},{9,8},{10,11... | collective-permute-start | bytes 1179656 | tf_op jit(solution)/shard_map/ppermute | solution.py:468
  13.7 7.7 %copy-start.2 = (bf16[32,8,1536]{2,1,0:T(8,128)(2,1)S(1)}, bf16[32,8,1536]{2,1,0:T(8,128)(2,1)}, u32[]{:S(2)}) copy-start(bf16[32,8,1536]{2,1,0:T(8,128)(2,1)} %depth_ref.5) | copy-start | bytes 2359300
  13.7 7.7 %copy-start.3 = (bf16[256,1536]{1,0:T(8,128)(2,1)S(1)}, bf16[256,1536]{1,0:T(8,128)(2,1)}, u32[]{:S(2)}) copy-start(bf16[256,1536]{1,0:T(8,128)(2,1)} %constant.65.clone.expand_ref) | copy-start | bytes 2359300
  22.3 26.0 %collective-permute-start.1 = (f32[2,32,1536]{2,1,0:T(8,128)S(1)}, f32[2,32,1536]{2,1,0:T(8,128)S(1)}, u32[]{:S(2)}, u32[]{:S(2)}) collective-permute-start(f32[2,32,1536]{2,1,0:T(8,128)S(1)} %get-tuple-element.8), channel_id=1, source_target_pairs={{0,2},{2,4},{4,6},{6,8},{8,10},{10,12},{12,14},{1,3},{3,5},{5,7},{... | collective-permute-start | bytes 1179656 | tf_op jit(solution)/shard_map/ppermute | solution.py:508
  26.9 21.5 %collective-permute-start.2 = (f32[2,32,1536]{2,1,0:T(8,128)S(1)}, f32[2,32,1536]{2,1,0:T(8,128)S(1)}, u32[]{:S(2)}, u32[]{:S(2)}) collective-permute-start(f32[2,32,1536]{2,1,0:T(8,128)S(1)} %get-tuple-element.7.sent_ref), channel_id=1, source_target_pairs={{2,0},{4,2},{6,4},{8,6},{10,8},{12,10},{14,12},{3,1},{5,3},{7,5},{... | collective-permute-start | bytes 1179656 | tf_op jit(solution)/shard_map/ppermute | solution.py:509
  29.4 18.9 %copy-start.5 = (f32[32]{0:T(128)S(1)}, f32[32]{0:T(128)}, u32[]{:S(2)}) copy-start(f32[32]{0:T(128)} %weight_ref.1) | copy-start | bytes 388
where the time goes:
time: 57.2 us; the launch traced here: 56.9 us
  Pallas kernels  40.3 us (70%)
  starting transfers between devices  8.78 us (15%)
  local copies, waits for them, and re-layouts  3.2 us (6%)
  other arithmetic  3.05 us (5%)
  waiting for transfers between devices  1.36 us (2%)
    pallas_call x1, Pallas kernels, on_pair(): pl.pallas_call(inner_kernel, grid=(rows // 2,), in_specs=[whole(flat), wh...  18.9 us
    pallas_call x1, Pallas kernels, on_pair(): pl.pallas_call(final_kernel, grid=(steps,), in_specs=[pl.BlockSpec(memory...  8.54 us
    pallas_call x1, Pallas kernels, on_pair(): pl.pallas_call(rim_kernel, grid=(1,), in_specs=[whole(flat), whole(around...  6.34 us
    pallas_call x1, Pallas kernels, on_pair(): pl.pallas_call(project_kernel, grid=(steps,), in_specs=[four, whole(trig)...  5.68 us
    ppermute x1, starting transfers between devices, on_pair(): lax.ppermute(last, 'lat', [(i, i + 1) for i in range(lat_count - 1)])  4.58 us
    unnamed x18, local copies, waits for them, and re-layouts  2.16 us
    ppermute x1, starting transfers between devices, on_pair(): lax.ppermute(first, 'lat', [(i + 1, i) for i in range(lat_count - 1)])  2.1 us
    ppermute x1, starting transfers between devices, on_pair(): arrived = lax.ppermute(z, 'lon', [(0, 1), (1, 0)])  2.1 us
  transfers between devices with their start and end apart: 3, of which 1 were waited for; matrix products, arithmetic and copies ran while one was open for 3% of the time, Pallas kernels for 44%

commit v1 on v0

v1 whole, which is shorter than its diff:
```python
import functools
import math

import jax
import jax.numpy as jnp
import ml_dtypes
import numpy as np
from jax import lax
from jax.experimental import pallas as pl
from jax.experimental.pallas import tpu as pltpu
from jax.sharding import PartitionSpec as P

KMAX = 1024
POLE_ROWS = 24


def extended(cells, sides, width, closed):
    for axis, dim in sides:
        count = lax.axis_size(axis)
        ends = count if closed else count - 1
        head = lax.slice_in_dim(cells, 0, width, axis=dim)
        tail = lax.slice_in_dim(cells, cells.shape[dim] - width, cells.shape[dim], axis=dim)
        cells = jnp.concatenate(
            [
                lax.ppermute(tail, axis, [(i, (i + 1) % count) for i in range(ends)]),
                cells,
                lax.ppermute(head, axis, [((i + 1) % count, i) for i in range(ends)]),
            ],
            axis=dim,
        )
    return cells


def entering(value, axis, join, neutral):
    count, mine = (lax.axis_size(axis), lax.axis_index(axis))
    pieces = lax.all_gather(value, axis)
    total = jnp.full_like(value, 0) + jnp.asarray(neutral, value.dtype)

    def turn(position, total):
        longer = join(total, pieces[position])
        return jnp.where(position < mine, longer, total)

    return lax.fori_loop(0, count - 1, turn, total)


def wave_table(col_count, wave_start, wave_count, circle):
    columns = lax.iota(jnp.int32, col_count)
    wave_index = wave_start + lax.iota(jnp.int32, wave_count)
    phase = columns[:, None] * wave_index[None, :] % circle
    angle = phase.astype(jnp.float32) * (2.0 * math.pi / circle)
    return jnp.concatenate([jnp.cos(angle), jnp.sin(angle)], axis=1)


def keep_weights(cut_rows, wave_start, wave_count, circle):
    wave_index = wave_start + lax.iota(jnp.int32, wave_count)
    factor = jnp.where(wave_index == 0, 1.0, 2.0) / circle
    kept = (wave_index[None, :] <= cut_rows[:, None]).astype(jnp.float32) * factor[None, :]
    return jnp.concatenate([kept, kept], axis=1)


def block_width():
    return min(KMAX, 128)


def project_rows(row_data, cut_rows):
    circle = row_data.shape[1]
    width = block_width()
    result = jnp.zeros(row_data.shape, jnp.float32)
    for block_index in range(KMAX // width):
        table = wave_table(circle, block_index * width, width, circle)
        coefs = jnp.dot(
            row_data, table, precision=lax.Precision.HIGHEST, preferred_element_type=jnp.float32
        )
        weights = keep_weights(cut_rows, block_index * width, width, circle)
        result = result + jnp.dot(
            coefs * weights,
            table.T,
            precision=lax.Precision.HIGHEST,
            preferred_element_type=jnp.float32,
        )
    return result


def transpose_filter(row_data, cut_rows, flag_rows):
    lon_count = lax.axis_size("lon")
    lon_index = lax.axis_index("lon")
    share = row_data.shape[0] // lon_count
    full_rows = lax.all_to_all(row_data, "lon", split_axis=0, concat_axis=1, tiled=True)
    my_cuts = lax.dynamic_slice_in_dim(cut_rows, lon_index * share, share)
    smoothed = project_rows(full_rows, my_cuts)
    returned = lax.all_to_all(smoothed, "lon", split_axis=1, concat_axis=0, tiled=True)
    return jnp.where(flag_rows[:, None] > 0, returned, row_data)


def polar_filter(row_data, cut_rows, flag_rows):
    return transpose_filter(row_data, cut_rows, flag_rows)


def on_device(adjoint, depth, zonal_coef, merid_coef, coriolis, layer_weight, cutoffs, polar_flags):
    fields, level_count, lat_rows, lon_cells = adjoint.shape
    lat_index = lax.axis_index("lat")
    lat_total = lat_rows * lax.axis_size("lat")
    stacked = adjoint.reshape(fields * level_count, lat_rows, lon_cells)
    bands = lax.all_to_all(stacked, "lat", split_axis=0, concat_axis=1, tiled=True)
    groups = bands.shape[0]
    polar_block = jnp.concatenate([bands[:, :POLE_ROWS], bands[:, lat_total - POLE_ROWS :]], axis=1)
    polar_cuts = jnp.concatenate([cutoffs[:POLE_ROWS], cutoffs[lat_total - POLE_ROWS :]])
    polar_marks = jnp.concatenate([polar_flags[:POLE_ROWS], polar_flags[lat_total - POLE_ROWS :]])
    row_data = polar_block.reshape(groups * 2 * POLE_ROWS, lon_cells)
    cut_rows = jnp.tile(polar_cuts, groups)
    flag_rows = jnp.tile(polar_marks, groups)
    treated = polar_filter(row_data, cut_rows, flag_rows)
    treated = treated.reshape(groups, 2 * POLE_ROWS, lon_cells)
    bands = jnp.concatenate(
        [
            treated[:, :POLE_ROWS],
            bands[:, POLE_ROWS : lat_total - POLE_ROWS],
            treated[:, POLE_ROWS:],
        ],
        axis=1,
    )
    filtered = lax.all_to_all(bands, "lat", split_axis=1, concat_axis=0, tiled=True).reshape(
        adjoint.shape
    )
    q_height = filtered[0]
    q_east = filtered[1]
    q_north = filtered[2]
    zonal_rows = lax.dynamic_slice_in_dim(zonal_coef, lat_index * lat_rows, lat_rows)[None, :, None]
    merid_rows = lax.dynamic_slice_in_dim(merid_coef, lat_index * lat_rows, lat_rows)[None, :, None]
    coriolis_rows = lax.dynamic_slice_in_dim(coriolis, lat_index * lat_rows, lat_rows)[
        None, :, None
    ]
    height_flux = depth.astype(jnp.float32) * q_height
    north_pair = jnp.stack([merid_rows * q_north, merid_rows * height_flux])
    north_rims = extended(north_pair, (("lat", 2),), 1, False)
    merid_diff = north_rims[:, :, :-2] - north_rims[:, :, 2:]
    east_pair = jnp.stack([q_east, height_flux])
    east_rims = extended(east_pair, (("lon", 3),), 1, True)
    zonal_diff = zonal_rows * (east_rims[..., :-2] - east_rims[..., 2:])
    column_force = -zonal_diff[0] - merid_diff[0]
    running = jnp.cumsum(column_force, axis=0)
    carried = entering(
        jnp.sum(column_force, axis=0), "lev", jnp.add, jnp.zeros((lat_rows, lon_cells), jnp.float32)
    )
    new_height = adjoint[0] + layer_weight[:, None, None] * (running + carried[None])
    new_east = adjoint[1] - zonal_diff[1] - coriolis_rows * q_north
    new_north = adjoint[2] - merid_diff[1] + coriolis_rows * q_east
    return jnp.stack([new_height, new_east, new_north])


REMOTE = 28
OWN = 28
OTHER = 30
FAR = 32
TILE = 256
LANES = 128
ROWS = 8
ORDER = (2, 0, 1)
MESH = pl.DeviceIdType.MESH


def halves(value):
    high = value.astype(jnp.bfloat16)
    return high, (value - high.astype(jnp.float32)).astype(jnp.bfloat16)


def split_table(value):
    high = np.asarray(value, np.float32).astype(ml_dtypes.bfloat16)
    low = (np.asarray(value, np.float32) - high.astype(np.float32)).astype(ml_dtypes.bfloat16)
    return high, low


def factors(matrix, rank):
    u, s, v = np.linalg.svd(matrix, full_matrices=False)
    size = np.sqrt(s[:rank])
    return u[:, :rank] * size, v[:rank].T * size


@functools.lru_cache(maxsize=None)
def kernel_tables(cells):
    circle = 2 * cells

    def kernel(distance):
        wave = circle * np.sin(np.pi * (distance % (2 * circle)) / circle)
        return np.where(distance % circle == 0, 0.0, 1.0 / np.where(distance % circle == 0, 1.0, wave))

    n = np.arange(cells)
    here = kernel(n[:, None] - n[None, :])
    project = np.zeros((cells, LANES))
    expand = np.zeros((LANES, cells))
    left, right = factors(kernel(n[:, None] - n[None, :] - cells), REMOTE)
    project[:, :REMOTE] = right
    expand[:REMOTE] = left.T
    project[:, OWN] = kernel(cells - 1 - n)
    project[:, OWN + 1] = kernel(0 - n)
    project[:, OTHER] = kernel(cells - 1 - n - cells)
    project[:, OTHER + 1] = kernel(0 - n - cells)
    blocks = cells // TILE
    at = FAR
    for block in range(blocks):
        part = slice(block * TILE, (block + 1) * TILE)
        far = here[part].copy()
        far[:, part] = 0.0
        rank = 12 if block in (0, blocks - 1) else 18
        left, right = factors(far, rank)
        project[:, at : at + rank] = right
        expand[at : at + rank, part] = left.T
        at += rank
    near = kernel(n[:TILE, None] - n[None, :TILE]).T
    project_high, project_low = split_table(project)
    expand_high, expand_low = split_table(expand)
    near_high, near_low = split_table(near)
    return (
        np.concatenate([project_high, project_low], axis=1),
        np.concatenate([expand_high, expand_high, expand_low]),
        np.concatenate([near_high, near_high, near_low]),
    )


def column(ref, first, kind=jnp.float32):
    row = lax.broadcasted_iota(jnp.int32, (ROWS, LANES), 0)
    value = jnp.zeros((ROWS, LANES), kind)
    for turn in range(ROWS):
        value = jnp.where(row == turn, ref[first + turn], value)
    return value


def across(value, width):
    return jnp.concatenate([value] * (width // LANES), axis=1)


def filter_kernel(
    merid_ref, cuts_ref, flags_ref, x_hbm, depth_hbm, project_hbm, expand_hbm, near_hbm,
    q_hbm, rims_ref, edges_ref,
    x_ref, depth_ref, project_ref, expand_ref, near_ref, high_ref, low_ref, code_ref, edge_ref, send_ref, take_ref,
    rows_ref, brink_ref, load_sem, table_sem, store_sem, out_sem, in_sem, up_sem, up_in_sem, down_sem, down_in_sem,
):
    fields, levels, rows, cells = x_ref.shape
    circle = 2 * cells
    count = levels * rows
    half = count // 2
    lat_count = lax.axis_size("lat")
    lat = lax.axis_index("lat")
    lon = lax.axis_index("lon")
    loads = [pltpu.make_async_copy(x_hbm.at[f], x_ref.at[f], load_sem.at[f]) for f in range(fields)]
    tables = [
        pltpu.make_async_copy(source, target, table_sem.at[turn])
        for turn, (source, target) in enumerate(
            ((project_hbm, project_ref), (depth_hbm, depth_ref), (near_hbm, near_ref), (expand_hbm, expand_ref))
        )
    ]
    loads[ORDER[0]].start()
    tables[0].start()
    loads[ORDER[1]].start()
    tables[1].start()
    loads[ORDER[2]].start()
    tables[2].start()
    tables[3].start()

    barrier = pltpu.get_barrier_semaphore()
    pl.semaphore_signal(barrier, inc=1, device_id={"lon": 1 - lon}, device_id_type=MESH)

    @pl.when(lat > 0)
    def _():
        pl.semaphore_signal(barrier, inc=1, device_id={"lat": lat - 1}, device_id_type=MESH)

    @pl.when(lat < lat_count - 1)
    def _():
        pl.semaphore_signal(barrier, inc=1, device_id={"lat": lat + 1}, device_id_type=MESH)

    first = lat * rows
    cuts = column(cuts_ref, first, jnp.int32)
    on = jnp.where(column(flags_ref, first, jnp.int32) > 0, 1.0, 0.0)
    merid = column(merid_ref, first)
    kept = (2 * cuts + 1).astype(jnp.float32)
    keep = jnp.where(on > 0.0, kept * (1.0 / circle), 1.0)
    odd = jnp.bitwise_and(cuts, 1)
    sign = on * jnp.where(odd == 0, -1.0, 1.0)
    place = lax.broadcasted_iota(jnp.int32, (rows, cells), 1).astype(jnp.float32)
    phase = across(kept, cells) * place
    phase = phase - jnp.floor(phase * (1.0 / (2 * circle))) * (2.0 * circle)
    angle = phase * (math.pi / circle)
    cos = across(on, cells) * jnp.cos(angle)
    sin = across(on, cells) * jnp.sin(angle)
    lane = lax.broadcasted_iota(jnp.int32, (rows, LANES), 1)

    def at_edges(end, start, low):
        return jnp.where(lane == low, end, jnp.where(lane == low + 1, start, 0.0))

    end_cos, end_sin = cos[:, cells - 1 :], sin[:, cells - 1 :]
    start_cos, start_sin = cos[:, :1], sin[:, :1]
    mix_cos = at_edges(end_sin, start_sin, OWN) + at_edges(sign * end_cos, sign * start_cos, OTHER)
    mix_sin = at_edges(-end_cos, -start_cos, OWN) + at_edges(sign * end_sin, sign * start_sin, OTHER)
    rows_ref[0] = cos
    rows_ref[1] = sin

    def exchange(field):
        return pltpu.make_async_remote_copy(
            src_ref=send_ref.at[field], dst_ref=take_ref.at[field], send_sem=out_sem.at[field],
            recv_sem=in_sem.at[field], device_id={"lon": 1 - lon}, device_id_type=MESH,
        )

    def spread(value):
        return jnp.broadcast_to(value[None], (levels,) + value.shape).reshape(count, value.shape[1])

    def climb(which):
        return pltpu.make_async_remote_copy(
            src_ref=brink_ref.at[1, which], dst_ref=edges_ref.at[0, which], send_sem=up_sem.at[which],
            recv_sem=up_in_sem.at[which], device_id={"lat": lat + 1}, device_id_type=MESH,
        )

    def descend(which):
        return pltpu.make_async_remote_copy(
            src_ref=brink_ref.at[0, which], dst_ref=edges_ref.at[1, which], send_sem=down_sem.at[which],
            recv_sem=down_in_sem.at[which], device_id={"lat": lat - 1}, device_id_type=MESH,
        )

    lane_all = lax.broadcasted_iota(jnp.int32, (count, LANES), 1)
    part = 8
    for turn, field in enumerate(ORDER):
        loads[field].wait()
        for group in range(levels // part):
            x = x_ref[field, group * part : (group + 1) * part]
            for which in range(2):
                high, low = halves((x * rows_ref[which][None]).reshape(part * rows, cells))
                at = slice(which * count + group * part * rows, which * count + (group + 1) * part * rows)
                high_ref[field, at] = high
                low_ref[field, at] = low
        if turn == 0:
            tables[0].wait()
        table = project_ref[...]
        total = jnp.dot(high_ref[field], table, preferred_element_type=jnp.float32)
        total = total + jnp.dot(low_ref[field], table, preferred_element_type=jnp.float32)
        code = total[:, :LANES] + total[:, LANES:]
        code_ref[field] = code
        code_cos, code_sin = code[:count], code[count:]
        message = jnp.where(lane_all < 32, code_cos, pltpu.roll(code_sin, 32, 1))
        if field < 2:
            edge = spread(mix_cos) * code_cos + spread(mix_sin) * code_sin
            start, end = x_ref[field, :, :, :LANES], x_ref[field, :, :, cells - LANES :]
            start, end = start.reshape(count, LANES)[:, :1], end.reshape(count, LANES)[:, LANES - 1 :]
            edge = edge + spread(keep) * jnp.where(lane_all == OWN, end, jnp.where(lane_all == OWN + 1, start, 0.0))
            edge_ref[field] = edge
            message = jnp.where(jnp.logical_and(lane_all >= OWN, lane_all < OWN + 2), edge, message)
        if field == 0:
            tables[1].wait()
            start, end = depth_ref[:, :, :LANES], depth_ref[:, :, cells - LANES :]
            start = start.astype(jnp.float32).reshape(count, LANES)[:, :1]
            end = end.astype(jnp.float32).reshape(count, LANES)[:, LANES - 1 :]
            message = jnp.where(lane_all == OWN + 32, end, jnp.where(lane_all == OWN + 33, start, message))
        send_ref[field] = jnp.where(lane_all[:half] < 64, message[:half], pltpu.roll(message[half:], 64, 1))
        if turn == 0:
            greeted = 1 + jnp.where(lat > 0, 1, 0) + jnp.where(lat < lat_count - 1, 1, 0)
            pl.semaphore_wait(barrier, greeted)
        exchange(field).start()

    @pl.when(lat == 0)
    def _():
        edges_ref[0] = jnp.zeros(edges_ref.shape[1:], jnp.float32)

    @pl.when(lat == lat_count - 1)
    def _():
        edges_ref[1] = jnp.zeros(edges_ref.shape[1:], jnp.float32)

    tables[2].wait()
    tables[3].wait()
    stores = []
    for field in ORDER:
        exchange(field).wait_recv()
        taken = take_ref[field]
        taken = jnp.concatenate([taken, pltpu.roll(taken, 64, 1)])
        turned = pltpu.roll(taken, 96, 1)
        if field < 2:
            rims = taken + pltpu.roll(edge_ref[field], LANES - 2, 1)
            if field == 0:
                rims = rims * turned
            rims_ref[field] = rims.reshape(levels, rows, LANES)
        signs = spread(sign)
        code = code_ref[field]
        code = jnp.concatenate(
            [
                jnp.where(lane_all < REMOTE, signs * turned, code[:count]),
                jnp.where(lane_all < REMOTE, -signs * taken, code[count:]),
            ]
        )
        code_high, code_low = halves(code)
        for block in range(cells // TILE):
            at = slice(block * TILE, (block + 1) * TILE)
            high, low = high_ref[field, :, at], low_ref[field, :, at]
            terms = jnp.concatenate([high, low, high, code_high, code_low, code_high], axis=1)
            weights = jnp.concatenate([near_ref[...], expand_ref[:, at]], axis=0)
            value = jnp.dot(terms, weights, preferred_element_type=jnp.float32)
            shape = (levels, rows, TILE)
            result = across(keep, TILE)[None] * x_ref[field, :, :, at]
            result = result + rows_ref[1, :, at][None] * value[:count].reshape(shape)
            result = result - rows_ref[0, :, at][None] * value[count:].reshape(shape)
            x_ref[field, :, :, at] = result
            if field != 1:
                edge = result
                if field == 0:
                    edge = result * depth_ref[:, :, at].astype(jnp.float32)
                edge = edge * across(merid, TILE)[None]
                which = 0 if field == 2 else 1
                brink_ref[0, which, :, at] = edge[:, 0, :]
                brink_ref[1, which, :, at] = edge[:, rows - 1, :]
        store = pltpu.make_async_copy(x_ref.at[field], q_hbm.at[field], store_sem.at[field])
        store.start()
        stores.append(store)
        if field != 1:
            which = 0 if field == 2 else 1

            @pl.when(lat < lat_count - 1)
            def _():
                climb(which).start()

            @pl.when(lat > 0)
            def _():
                descend(which).start()

    for store in stores:
        store.wait()
    for field in ORDER:
        exchange(field).wait_send()

    @pl.when(lat < lat_count - 1)
    def _():
        for which in range(2):
            climb(which).wait_send()
            descend(which).wait_recv()

    @pl.when(lat > 0)
    def _():
        for which in range(2):
            descend(which).wait_send()
            climb(which).wait_recv()


def final_kernel(
    zonal_ref, merid_ref, coriolis_ref, weight_ref, x_ref, q_ref, depth_ref, edges_ref, rims_ref, out_ref, run_ref
):
    step = pl.program_id(0)
    _, levels, rows, cells = x_ref.shape
    first = lax.axis_index("lat") * rows
    zonal = across(column(zonal_ref, first), cells)
    merid = across(column(merid_ref, first), cells)
    coriolis = across(column(coriolis_ref, first), cells)
    row = lax.broadcasted_iota(jnp.int32, (rows, cells), 0)
    lane = lax.broadcasted_iota(jnp.int32, (rows, cells), 1)

    def zonal_adjoint(value, west, east):
        left = jnp.where(lane == 0, west, pltpu.roll(value, 1, 1))
        right = jnp.where(lane == cells - 1, east, pltpu.roll(value, cells - 1, 1))
        return zonal * (left - right)

    def merid_adjoint(value, before, after):
        value = merid * value
        up = jnp.where(row == 0, before, pltpu.roll(value, 1, 0))
        down = jnp.where(row == rows - 1, after, pltpu.roll(value, rows - 1, 0))
        return up - down

    @pl.when(step == 0)
    def _():
        run_ref[...] = jnp.zeros_like(run_ref)

    run = run_ref[...]
    for level in range(levels):
        height, east, north = q_ref[0, level], q_ref[1, level], q_ref[2, level]
        flux = depth_ref[level].astype(jnp.float32) * height
        line = pl.ds(level, 1)
        flux_rims, east_rims = rims_ref[0, level], rims_ref[1, level]
        run = run - (
            zonal_adjoint(east, east_rims[:, OWN : OWN + 1], east_rims[:, OWN + 1 : OWN + 2])
            + merid_adjoint(north, edges_ref[0, 0, line, :], edges_ref[1, 0, line, :])
        )
        out_ref[0, level] = x_ref[0, level] + weight_ref[step * levels + level] * run
        out_ref[1, level] = (
            x_ref[1, level]
            - zonal_adjoint(flux, flux_rims[:, OWN : OWN + 1], flux_rims[:, OWN + 1 : OWN + 2])
            - coriolis * north
        )
        out_ref[2, level] = (
            x_ref[2, level]
            - merid_adjoint(flux, edges_ref[0, 1, line, :], edges_ref[1, 1, line, :])
            + coriolis * east
        )
    run_ref[...] = run


def on_pair(adjoint, depth, zonal_coef, merid_coef, coriolis, layer_weight, cutoffs, polar_flags):
    fields, level_count, rows, cells = adjoint.shape
    project, expand, near = (jnp.asarray(table) for table in kernel_tables(cells))
    count = level_count * rows
    scalars = pl.BlockSpec(memory_space=pltpu.SMEM)
    there = pl.BlockSpec(memory_space=pl.ANY)
    close = pl.BlockSpec(memory_space=pltpu.VMEM)
    single = jnp.float32
    dma = pltpu.SemaphoreType.DMA

    q, rims, edges = pl.pallas_call(
        filter_kernel,
        in_specs=[scalars] * 3 + [there] * 5,
        out_specs=[there, close, close],
        out_shape=[
            jax.ShapeDtypeStruct(adjoint.shape, single),
            jax.ShapeDtypeStruct((2, level_count, rows, LANES), single),
            jax.ShapeDtypeStruct((2, 2, level_count, cells), single),
        ],
        scratch_shapes=[
            pltpu.VMEM(adjoint.shape, single),
            pltpu.VMEM(depth.shape, depth.dtype),
            pltpu.VMEM(project.shape, project.dtype),
            pltpu.VMEM(expand.shape, expand.dtype),
            pltpu.VMEM(near.shape, near.dtype),
            pltpu.VMEM((fields, 2 * count, cells), jnp.bfloat16),
            pltpu.VMEM((fields, 2 * count, cells), jnp.bfloat16),
            pltpu.VMEM((fields, 2 * count, LANES), single),
            pltpu.VMEM((2, count, LANES), single),
            pltpu.VMEM((fields, count // 2, LANES), single),
            pltpu.VMEM((fields, count // 2, LANES), single),
            pltpu.VMEM((2, rows, cells), single),
            pltpu.VMEM((2, 2, level_count, cells), single),
            dma((3,)),
            dma((4,)),
            dma((3,)),
            dma((3,)),
            dma((3,)),
            dma((2,)),
            dma((2,)),
            dma((2,)),
            dma((2,)),
        ],
        compiler_params=pltpu.CompilerParams(
            collective_id=0, has_side_effects=True, vmem_limit_bytes=48 * 2**20
        ),
    )(merid_coef, cutoffs, polar_flags, adjoint, depth, project, expand, near)

    part = 8
    four = pl.BlockSpec((fields, part, rows, cells), lambda i: (0, i, 0, 0))
    three = pl.BlockSpec((part, rows, cells), lambda i: (i, 0, 0))
    return pl.pallas_call(
        final_kernel,
        grid=(level_count // part,),
        in_specs=[scalars] * 4
        + [
            four,
            four,
            three,
            pl.BlockSpec((2, 2, part, cells), lambda i: (0, 0, i, 0)),
            pl.BlockSpec((2, part, rows, LANES), lambda i: (0, i, 0, 0)),
        ],
        out_specs=four,
        out_shape=jax.ShapeDtypeStruct(adjoint.shape, single),
        scratch_shapes=[pltpu.VMEM((rows, cells), single)],
        compiler_params=pltpu.CompilerParams(vmem_limit_bytes=32 * 2**20),
    )(zonal_coef, merid_coef, coriolis, layer_weight, adjoint, q, depth, edges, rims)


def plan_for(mesh):
    return on_pair if mesh.shape["lon"] == 2 and mesh.shape["lev"] == 1 else on_device


def solution(mesh):
    return jax.shard_map(
        plan_for(mesh),
        mesh=mesh,
        in_specs=(
            P("member", "lev", "lat", "lon"),
            P("lev", "lat", "lon"),
            P(),
            P(),
            P(),
            P("lev"),
            P(),
            P(),
        ),
        out_specs=P("member", "lev", "lat", "lon"),
        check_vma=False,
    )
```

time: 57.2 us -> 34.3 us (0.60)
  Pallas kernels: 40.3 us -> 24.7 us
  starting transfers between devices: 8.78 us -> 0 us
  local copies, waits for them, and re-layouts: 3.2 us -> 9.28 us
  other arithmetic: 3.05 us -> 0 us
  waiting for transfers between devices: 1.36 us -> 0 us
    pallas_call x5 -> x2, Pallas kernels: 40.3 us -> 24.7 us  [the longest x1 19.9 us: on_pair(): pl.pallas_call(filter_kernel, in_specs=[scalars] * 3 + [there] * 5, out_s...]
    ppermute x3 -> x0, starting transfers between devices: 8.78 us -> none  [the longest x1 4.58 us: on_pair(): lax.ppermute(last, 'lat', [(i, i + 1) for i in range(lat_count - 1)])]
    unnamed x18 -> x24, local copies, waits for them, and re-layouts: 2.16 us -> 9.28 us
    ppermute x3 -> x0, waiting for transfers between devices: 1.36 us -> none  [the longest x1 1.36 us: on_pair(): arrived = lax.ppermute(z, 'lon', [(0, 1), (1, 0)])]
    cos x2 -> x0, other arithmetic: 0.95 us -> none  [on_pair(): cos, sin = (jnp.cos(angle), jnp.sin(angle))]
    another operation x6 -> x0, other arithmetic: 0.88 us -> none  [the longest x1 0.77 us: on_pair(): edge = keep[None]]
    mul x2 -> x0, other arithmetic: 0.81 us -> none  [the longest x1 0.74 us: on_pair(): sign = on * jnp.where(cuts % 2 == 0, -1.0, 1.0)[:, None]]
  transfers between devices with their start and end apart: 3 -> 0, of which waited for: 1 -> 0; matrix products, arithmetic and copies ran while one was open for 3% -> 0% of each run, Pallas kernels for 44% -> 0%
where the time goes in v1:
time: 34.3 us; the launch traced here: 34.1 us
  Pallas kernels  24.7 us (72%)
  local copies, waits for them, and re-layouts  9.28 us (27%)
    pallas_call x1, Pallas kernels, on_pair(): pl.pallas_call(filter_kernel, in_specs=[scalars] * 3 + [there] * 5, out_s...  19.9 us
    unnamed x24, local copies, waits for them, and re-layouts  9.28 us
    pallas_call x1, Pallas kernels, on_pair(): pl.pallas_call(final_kernel, grid=(level_count // part,), in_specs=[scala...  4.82 us

profile of v1, /device:TPU:1, one launch (start us, length us, event | category | flops | bytes accessed | tf_op | source)
XLA Modules:
  0.0 34.1 jit_solution(5408102857247574139)
XLA Ops:
  0.0 0.0 copy-start
  0.0 0.0 copy-start.2
  0.0 1.3 %copy-done.2 = bf16[32,8,1536]{2,1,0:T(8,128)(2,1)S(1)} copy-done((bf16[32,8,1536]{2,1,0:T(8,128)(2,1)S(1)}, bf16[32,8,1536]{2,1,0:T(8,128)(2,1)}, u32[]{:S(2)}) %copy-start.2) | copy-done | bytes 786456
  1.3 0.0 copy-start.3
  1.3 1.6 %copy-done.3 = bf16[384,1536]{1,0:T(8,128)(2,1)S(1)} copy-done((bf16[384,1536]{1,0:T(8,128)(2,1)S(1)}, bf16[384,1536]{1,0:T(8,128)(2,1)}, u32[]{:S(2)}) %copy-start.3) | copy-done | bytes 1179672
  2.8 0.0 copy-start.4
  2.8 1.1 %copy-done.4 = bf16[1536,256]{1,0:T(8,128)(2,1)S(1)} copy-done((bf16[1536,256]{1,0:T(8,128)(2,1)S(1)}, bf16[1536,256]{1,0:T(8,128)(2,1)}, u32[]{:S(2)}) %copy-start.4) | copy-done | bytes 786456
  4.0 0.0 copy-start.5
  4.0 1.0 %copy-done.5 = bf16[768,256]{1,0:T(8,128)(2,1)S(1)} copy-done((bf16[768,256]{1,0:T(8,128)(2,1)S(1)}, bf16[768,256]{1,0:T(8,128)(2,1)}, u32[]{:S(2)}) %copy-start.5) | copy-done | bytes 393240
  5.0 0.0 copy-start.6
  5.0 0.7 %copy-done.6 = f32[64]{0:T(128)S(1)} copy-done((f32[64]{0:T(128)S(1)}, f32[64]{0:T(128)}, u32[]{:S(2)}) %copy-start.6) | copy-done | bytes 280
  5.6 0.0 copy-start.7
  5.6 0.7 %copy-done.7 = s32[64]{0:T(128)S(1)} copy-done((s32[64]{0:T(128)S(1)}, s32[64]{0:T(128)}, u32[]{:S(2)}) %copy-start.7) | copy-done | bytes 280
  6.3 0.0 copy-start.8
  6.3 0.7 %copy-done.8 = s32[64]{0:T(128)S(1)} copy-done((s32[64]{0:T(128)S(1)}, s32[64]{0:T(128)}, u32[]{:S(2)}) %copy-start.8) | copy-done | bytes 280
  6.9 0.0 copy-start.9
  6.9 0.0 copy-start.10
  6.9 0.0 copy-start.11
  6.9 19.9 %shard_map.109 = (f32[3,32,8,1536]{3,2,1,0:T(8,128)}, f32[2,32,8,128]{3,2,1,0:T(8,128)S(1)}, f32[2,2,32,1536]{3,2,1,0:T(8,128)S(1)}) custom-call(f32[64]{0:T(128)S(1)} %copy-done.6, s32[64]{0:T(128)S(1)} %copy-done.7, s32[64]{0:T(128)S(1)} %copy-done.8, f32[3,32,8,1536]{3,2,1,0:T(8,128)} %x_ref.1, bf16[32,8,1536]{2,1,0:T(8,128)(2,1)S(1)} %copy-done.2, ...), custom_call_target="tpu_custom_call" | custom-call | tf_op jit(solution)/shard_map/pallas_call | solution.py:499
  26.9 0.0 copy-done
  26.9 0.0 copy-done.9
  26.9 0.0 copy-done.10
  26.9 0.0 copy-done.11
  26.9 0.0 copy-start.1
  26.9 2.3 %copy-done.1 = f32[3,32,8,1536]{3,2,1,0:T(8,128)S(1)} copy-done((f32[3,32,8,1536]{3,2,1,0:T(8,128)S(1)}, f32[3,32,8,1536]{3,2,1,0:T(8,128)}, u32[]{:S(2)}) %copy-start.1) | copy-done | bytes 4718616
  29.2 4.8 %shard_map.110 = f32[3,32,8,1536]{3,2,1,0:T(8,128)} custom-call(f32[64]{0:T(128)S(1)} %copy-done.9, f32[64]{0:T(128)S(1)} %copy-done.6, f32[64]{0:T(128)S(1)} %copy-done.10, f32[32]{0:T(128)S(1)} %copy-done.11, f32[3,32,8,1536]{3,2,1,0:T(8,128)S(1)} %copy-done, f32[3,32,8,1536]{3,2,1,0:T(8,128)S(1)} %copy-done.1, bf16[32,8,1536]{2,1,0:T(8,128)(2,1)S(1)} %copy-done.2, ...), custom_call_target="tpu_custom_call" | custom-call | tf_op jit(solution)/shard_map/pallas_call | solution.py:540
Async XLA Ops:
  0.0 26.9 %copy-start = (f32[3,32,8,1536]{3,2,1,0:T(8,128)S(1)}, f32[3,32,8,1536]{3,2,1,0:T(8,128)}, u32[]{:S(2)}) copy-start(f32[3,32,8,1536]{3,2,1,0:T(8,128)} %x_ref.1) | copy-start | bytes 14155780
  0.0 1.3 %copy-start.2 = (bf16[32,8,1536]{2,1,0:T(8,128)(2,1)S(1)}, bf16[32,8,1536]{2,1,0:T(8,128)(2,1)}, u32[]{:S(2)}) copy-start(bf16[32,8,1536]{2,1,0:T(8,128)(2,1)} %depth_ref.1) | copy-start | bytes 2359300
  1.3 1.6 %copy-start.3 = (bf16[384,1536]{1,0:T(8,128)(2,1)S(1)}, bf16[384,1536]{1,0:T(8,128)(2,1)}, u32[]{:S(2)}) copy-start(bf16[384,1536]{1,0:T(8,128)(2,1)} %constant.7.clone.expand_hbm) | copy-start | bytes 3538948
  2.8 1.1 %copy-start.4 = (bf16[1536,256]{1,0:T(8,128)(2,1)S(1)}, bf16[1536,256]{1,0:T(8,128)(2,1)}, u32[]{:S(2)}) copy-start(bf16[1536,256]{1,0:T(8,128)(2,1)} %constant.6.clone.project_hbm) | copy-start | bytes 2359300
  4.0 1.0 %copy-start.5 = (bf16[768,256]{1,0:T(8,128)(2,1)S(1)}, bf16[768,256]{1,0:T(8,128)(2,1)}, u32[]{:S(2)}) copy-start(bf16[768,256]{1,0:T(8,128)(2,1)} %constant.8.clone.near_hbm) | copy-start | bytes 1179652
  5.0 0.7 %copy-start.6 = (f32[64]{0:T(128)S(1)}, f32[64]{0:T(128)}, u32[]{:S(2)}) copy-start(f32[64]{0:T(128)} %merid_ref.3) | copy-start | bytes 772
  5.6 0.7 %copy-start.7 = (s32[64]{0:T(128)S(1)}, s32[64]{0:T(128)}, u32[]{:S(2)}) copy-start(s32[64]{0:T(128)} %cuts_ref.1) | copy-start | bytes 772
  6.3 0.7 %copy-start.8 = (s32[64]{0:T(128)S(1)}, s32[64]{0:T(128)}, u32[]{:S(2)}) copy-start(s32[64]{0:T(128)} %flags_ref.1) | copy-start | bytes 772
  6.9 19.9 %copy-start.9 = (f32[64]{0:T(128)S(1)}, f32[64]{0:T(128)}, u32[]{:S(2)}) copy-start(f32[64]{0:T(128)} %zonal_ref.1) | copy-start | bytes 772
  6.9 19.9 %copy-start.10 = (f32[64]{0:T(128)S(1)}, f32[64]{0:T(128)}, u32[]{:S(2)}) copy-start(f32[64]{0:T(128)} %coriolis_ref.1) | copy-start | bytes 772
  6.9 19.9 %copy-start.11 = (f32[32]{0:T(128)S(1)}, f32[32]{0:T(128)}, u32[]{:S(2)}) copy-start(f32[32]{0:T(128)} %weight_ref.1) | copy-start | bytes 388
  26.9 2.3 %copy-start.1 = (f32[3,32,8,1536]{3,2,1,0:T(8,128)S(1)}, f32[3,32,8,1536]{3,2,1,0:T(8,128)}, u32[]{:S(2)}) copy-start(f32[3,32,8,1536]{3,2,1,0:T(8,128)} %get-tuple-element.8.q_ref) | copy-start | bytes 14155780

commit v2 on v1

--- a/solution.py
+++ b/solution.py
@@ -230,10 +230,10 @@
 
 
 def filter_kernel(
-    merid_ref, cuts_ref, flags_ref, x_hbm, depth_hbm, project_hbm, expand_hbm, near_hbm,
-    q_hbm, rims_ref, edges_ref,
-    x_ref, depth_ref, project_ref, expand_ref, near_ref, high_ref, low_ref, code_ref, edge_ref, send_ref, take_ref,
-    rows_ref, brink_ref, load_sem, table_sem, store_sem, out_sem, in_sem, up_sem, up_in_sem, down_sem, down_in_sem,
+    merid_hbm, cuts_hbm, flags_hbm, x_hbm, depth_hbm, project_hbm, expand_hbm, near_hbm,
+    q_ref, rims_ref, edges_ref,
+    merid_ref, cuts_ref, flags_ref, x_ref, depth_ref, project_ref, expand_ref, near_ref, high_ref, low_ref, code_ref, edge_ref, send_ref, take_ref,
+    rows_ref, brink_ref, scalar_sem, load_sem, table_sem, out_sem, in_sem, up_sem, up_in_sem, down_sem, down_in_sem,
 ):
     fields, levels, rows, cells = x_ref.shape
     circle = 2 * cells
@@ -242,6 +242,14 @@
     lat_count = lax.axis_size("lat")
     lat = lax.axis_index("lat")
     lon = lax.axis_index("lon")
+    scalars = [
+        pltpu.make_async_copy(source, target, scalar_sem.at[turn])
+        for turn, (source, target) in enumerate(
+            ((cuts_hbm, cuts_ref), (flags_hbm, flags_ref), (merid_hbm, merid_ref))
+        )
+    ]
+    for scalar in scalars:
+        scalar.start()
     loads = [pltpu.make_async_copy(x_hbm.at[f], x_ref.at[f], load_sem.at[f]) for f in range(fields)]
     tables = [
         pltpu.make_async_copy(source, target, table_sem.at[turn])
@@ -268,6 +276,8 @@
     def _():
         pl.semaphore_signal(barrier, inc=1, device_id={"lat": lat + 1}, device_id_type=MESH)
 
+    for scalar in scalars:
+        scalar.wait()
     first = lat * rows
     cuts = column(cuts_ref, first, jnp.int32)
     on = jnp.where(column(flags_ref, first, jnp.int32) > 0, 1.0, 0.0)
@@ -364,7 +374,6 @@
 
     tables[2].wait()
     tables[3].wait()
-    stores = []
     for field in ORDER:
         exchange(field).wait_recv()
         taken = take_ref[field]
@@ -394,7 +403,7 @@
             result = across(keep, TILE)[None] * x_ref[field, :, :, at]
             result = result + rows_ref[1, :, at][None] * value[:count].reshape(shape)
             result = result - rows_ref[0, :, at][None] * value[count:].reshape(shape)
-            x_ref[field, :, :, at] = result
+            q_ref[field, :, :, at] = result
             if field != 1:
                 edge = result
                 if field == 0:
@@ -403,9 +412,6 @@
                 which = 0 if field == 2 else 1
                 brink_ref[0, which, :, at] = edge[:, 0, :]
                 brink_ref[1, which, :, at] = edge[:, rows - 1, :]
-        store = pltpu.make_async_copy(x_ref.at[field], q_hbm.at[field], store_sem.at[field])
-        store.start()
-        stores.append(store)
         if field != 1:
             which = 0 if field == 2 else 1
 
@@ -417,8 +423,6 @@
             def _():
                 descend(which).start()
 
-    for store in stores:
-        store.wait()
     for field in ORDER:
         exchange(field).wait_send()
 
@@ -439,7 +443,7 @@
     zonal_ref, merid_ref, coriolis_ref, weight_ref, x_ref, q_ref, depth_ref, edges_ref, rims_ref, out_ref, run_ref
 ):
     step = pl.program_id(0)
-    _, levels, rows, cells = x_ref.shape
+    _, levels, rows, cells = out_ref.shape
     first = lax.axis_index("lat") * rows
     zonal = across(column(zonal_ref, first), cells)
     merid = across(column(merid_ref, first), cells)
@@ -463,7 +467,8 @@
         run_ref[...] = jnp.zeros_like(run_ref)
 
     run = run_ref[...]
-    for level in range(levels):
+    for turn in range(levels):
+        level = step * levels + turn
         height, east, north = q_ref[0, level], q_ref[1, level], q_ref[2, level]
         flux = depth_ref[level].astype(jnp.float32) * height
         line = pl.ds(level, 1)
@@ -472,13 +477,13 @@
             zonal_adjoint(east, east_rims[:, OWN : OWN + 1], east_rims[:, OWN + 1 : OWN + 2])
             + merid_adjoint(north, edges_ref[0, 0, line, :], edges_ref[1, 0, line, :])
         )
-        out_ref[0, level] = x_ref[0, level] + weight_ref[step * levels + level] * run
-        out_ref[1, level] = (
+        out_ref[0, turn] = x_ref[0, level] + weight_ref[level] * run
+        out_ref[1, turn] = (
             x_ref[1, level]
             - zonal_adjoint(flux, flux_rims[:, OWN : OWN + 1], flux_rims[:, OWN + 1 : OWN + 2])
             - coriolis * north
         )
-        out_ref[2, level] = (
+        out_ref[2, turn] = (
             x_ref[2, level]
             - merid_adjoint(flux, edges_ref[0, 1, line, :], edges_ref[1, 1, line, :])
             + coriolis * east
@@ -491,21 +496,24 @@
     project, expand, near = (jnp.asarray(table) for table in kernel_tables(cells))
     count = level_count * rows
     scalars = pl.BlockSpec(memory_space=pltpu.SMEM)
-    there = pl.BlockSpec(memory_space=pl.ANY)
+    there = pl.BlockSpec(memory_space=pltpu.HBM)
     close = pl.BlockSpec(memory_space=pltpu.VMEM)
     single = jnp.float32
     dma = pltpu.SemaphoreType.DMA
 
     q, rims, edges = pl.pallas_call(
         filter_kernel,
-        in_specs=[scalars] * 3 + [there] * 5,
-        out_specs=[there, close, close],
+        in_specs=[there] * 8,
+        out_specs=[close] * 3,
         out_shape=[
             jax.ShapeDtypeStruct(adjoint.shape, single),
             jax.ShapeDtypeStruct((2, level_count, rows, LANES), single),
             jax.ShapeDtypeStruct((2, 2, level_count, cells), single),
         ],
         scratch_shapes=[
+            pltpu.SMEM(merid_coef.shape, single),
+            pltpu.SMEM(cutoffs.shape, jnp.int32),
+            pltpu.SMEM(polar_flags.shape, jnp.int32),
             pltpu.VMEM(adjoint.shape, single),
             pltpu.VMEM(depth.shape, depth.dtype),
             pltpu.VMEM(project.shape, project.dtype),
@@ -520,8 +528,8 @@
             pltpu.VMEM((2, rows, cells), single),
             pltpu.VMEM((2, 2, level_count, cells), single),
             dma((3,)),
+            dma((3,)),
             dma((4,)),
-            dma((3,)),
             dma((3,)),
             dma((3,)),
             dma((2,)),
@@ -530,24 +538,16 @@
             dma((2,)),
         ],
         compiler_params=pltpu.CompilerParams(
-            collective_id=0, has_side_effects=True, vmem_limit_bytes=48 * 2**20
+            collective_id=0, has_side_effects=True, vmem_limit_bytes=36 * 2**20
         ),
-    )(merid_coef, cutoffs, polar_flags, adjoint, depth, project, expand, near)
+    )(*(pltpu.with_memory_space_constraint(value, pltpu.HBM) for value in (merid_coef, cutoffs, polar_flags, adjoint, depth, project, expand, near)))
 
     part = 8
     four = pl.BlockSpec((fields, part, rows, cells), lambda i: (0, i, 0, 0))
-    three = pl.BlockSpec((part, rows, cells), lambda i: (i, 0, 0))
     return pl.pallas_call(
         final_kernel,
         grid=(level_count // part,),
-        in_specs=[scalars] * 4
-        + [
-            four,
-            four,
-            three,
-            pl.BlockSpec((2, 2, part, cells), lambda i: (0, 0, i, 0)),
-            pl.BlockSpec((2, part, rows, LANES), lambda i: (0, i, 0, 0)),
-        ],
+        in_specs=[scalars] * 4 + [close] * 5,
         out_specs=four,
         out_shape=jax.ShapeDtypeStruct(adjoint.shape, single),
         scratch_shapes=[pltpu.VMEM((rows, cells), single)],

time: 34.3 us -> 24.4 us (0.71)
  local copies, waits for them, and re-layouts: 9.28 us -> 0.02 us
  Pallas kernels: 24.7 us -> 24.2 us
    unnamed x24 -> x12, local copies, waits for them, and re-layouts: 9.28 us -> 0.02 us
    pallas_call x1, Pallas kernels: 4.82 us -> 4.46 us  [on_pair(): pl.pallas_call(final_kernel, grid=(level_count // part,), in_specs=[scala...]
where the time goes in v2:
time: 24.4 us; the launch traced here: 24.3 us
  Pallas kernels  24.2 us (99%)
    pallas_call x1, Pallas kernels, on_pair(): pl.pallas_call(filter_kernel, in_specs=[there] * 8, out_specs=[close] * 3...  19.7 us
    pallas_call x1, Pallas kernels, on_pair(): pl.pallas_call(final_kernel, grid=(level_count // part,), in_specs=[scala...  4.46 us

profile of v2, /device:TPU:1, one launch (start us, length us, event | category | flops | bytes accessed | tf_op | source)
XLA Modules:
  0.0 24.3 jit_solution(16812103854768077316)
XLA Ops:
  0.0 0.0 copy-start.2
  0.0 0.0 copy-start.1
  0.0 0.0 copy-start
  0.0 0.0 copy-start.5
  0.0 0.0 copy-start.4
  0.0 0.0 copy-start.3
  0.0 19.7 %shard_map.109 = (f32[3,32,8,1536]{3,2,1,0:T(8,128)S(1)}, f32[2,32,8,128]{3,2,1,0:T(8,128)S(1)}, f32[2,2,32,1536]{3,2,1,0:T(8,128)S(1)}) custom-call(f32[64]{0:T(128)} %merid_ref.1, s32[64]{0:T(128)} %cuts_hbm.1, s32[64]{0:T(128)} %flags_hbm.1, f32[3,32,8,1536]{3,2,1,0:T(8,128)} %x_ref.1, bf16[32,8,1536]{2,1,0:T(8,128)(2,1)} %depth_ref.1, ...), custom_call_target="tpu_custom_call" | custom-call | tf_op jit(solution)/shard_map/pallas_call | solution.py:504
  19.8 0.0 copy-done.2
  19.8 0.0 copy-done.1
  19.8 0.0 copy-done
  19.8 0.0 copy-done.5
  19.8 0.0 copy-done.4
  19.8 0.0 copy-done.3
  19.8 4.5 %shard_map.110 = f32[3,32,8,1536]{3,2,1,0:T(8,128)} custom-call(f32[64]{0:T(128)S(1)} %copy-done.3, f32[64]{0:T(128)S(1)} %copy-done.2, f32[64]{0:T(128)S(1)} %copy-done.4, f32[32]{0:T(128)S(1)} %copy-done.5, f32[3,32,8,1536]{3,2,1,0:T(8,128)S(1)} %copy-done, f32[3,32,8,1536]{3,2,1,0:T(8,128)S(1)} %get-tuple-element.8.q_ref, ...), custom_call_target="tpu_custom_call" | custom-call | tf_op jit(solution)/shard_map/pallas_call | solution.py:547
Async XLA Ops:
  0.0 19.8 %copy-start.2 = (f32[64]{0:T(128)S(1)}, f32[64]{0:T(128)}, u32[]{:S(2)}) copy-start(f32[64]{0:T(128)} %merid_ref.1) | copy-start | bytes 772
  0.0 19.8 %copy-start.1 = (bf16[32,8,1536]{2,1,0:T(8,128)(2,1)S(1)}, bf16[32,8,1536]{2,1,0:T(8,128)(2,1)}, u32[]{:S(2)}) copy-start(bf16[32,8,1536]{2,1,0:T(8,128)(2,1)} %depth_ref.1) | copy-start | bytes 2359300
  0.0 19.8 %copy-start = (f32[3,32,8,1536]{3,2,1,0:T(8,128)S(1)}, f32[3,32,8,1536]{3,2,1,0:T(8,128)}, u32[]{:S(2)}) copy-start(f32[3,32,8,1536]{3,2,1,0:T(8,128)} %x_ref.1) | copy-start | bytes 14155780
  0.0 19.8 %copy-start.5 = (f32[32]{0:T(128)S(1)}, f32[32]{0:T(128)}, u32[]{:S(2)}) copy-start(f32[32]{0:T(128)} %weight_ref.1) | copy-start | bytes 388
  0.0 19.8 %copy-start.4 = (f32[64]{0:T(128)S(1)}, f32[64]{0:T(128)}, u32[]{:S(2)}) copy-start(f32[64]{0:T(128)} %coriolis_ref.1) | copy-start | bytes 772
  0.0 19.8 %copy-start.3 = (f32[64]{0:T(128)S(1)}, f32[64]{0:T(128)}, u32[]{:S(2)}) copy-start(f32[64]{0:T(128)} %zonal_ref.1) | copy-start | bytes 772

commit v3 on v2

--- a/solution.py
+++ b/solution.py
@@ -152,6 +152,8 @@
 OWN = 28
 OTHER = 30
 FAR = 32
+CODES = 80
+GROUP = 2
 TILE = 256
 LANES = 128
 ROWS = 8
@@ -206,13 +208,18 @@
         project[:, at : at + rank] = right
         expand[at : at + rank, part] = left.T
         at += rank
+    split = cells // 2
+    turned = np.roll(expand, 48, axis=0)
+    groups = []
+    for part in (expand[:CODES, :split], turned[:CODES, split:]):
+        high, low = split_table(part)
+        groups.append(np.concatenate([high, high, low, np.zeros((TILE - 3 * CODES, split), high.dtype)]))
     near = kernel(n[:TILE, None] - n[None, :TILE]).T
     project_high, project_low = split_table(project)
-    expand_high, expand_low = split_table(expand)
     near_high, near_low = split_table(near)
     return (
         np.concatenate([project_high, project_low], axis=1),
-        np.concatenate([expand_high, expand_high, expand_low]),
+        np.concatenate(groups, axis=1),
         np.concatenate([near_high, near_high, near_low]),
     )
 
@@ -231,9 +238,9 @@
 
 def filter_kernel(
     merid_hbm, cuts_hbm, flags_hbm, x_hbm, depth_hbm, project_hbm, expand_hbm, near_hbm,
-    q_ref, rims_ref, edges_ref,
-    merid_ref, cuts_ref, flags_ref, x_ref, depth_ref, project_ref, expand_ref, near_ref, high_ref, low_ref, code_ref, edge_ref, send_ref, take_ref,
-    rows_ref, brink_ref, scalar_sem, load_sem, table_sem, out_sem, in_sem, up_sem, up_in_sem, down_sem, down_in_sem,
+    q_ref, rims_ref, edges_ref, x_ref, depth_ref,
+    merid_ref, cuts_ref, flags_ref, project_ref, expand_ref, near_ref, high_ref, low_ref, code_ref, edge_ref, send_ref, take_ref,
+    rows_ref, brink_ref, scalar_sem, load_sem, table_sem, out_sem, in_sem, leave_sem, reach_sem,
 ):
     fields, levels, rows, cells = x_ref.shape
     circle = 2 * cells
@@ -268,20 +275,24 @@
     barrier = pltpu.get_barrier_semaphore()
     pl.semaphore_signal(barrier, inc=1, device_id={"lon": 1 - lon}, device_id_type=MESH)
 
-    @pl.when(lat > 0)
-    def _():
-        pl.semaphore_signal(barrier, inc=1, device_id={"lat": lat - 1}, device_id_type=MESH)
-
-    @pl.when(lat < lat_count - 1)
-    def _():
-        pl.semaphore_signal(barrier, inc=1, device_id={"lat": lat + 1}, device_id_type=MESH)
+    up = {"lat": jnp.minimum(lat + 1, lat_count - 1), "lon": jnp.where(lat < lat_count - 1, lon, 1 - lon)}
+    down = {"lat": jnp.maximum(lat - 1, 0), "lon": jnp.where(lat > 0, lon, 1 - lon)}
+    upward = [lat % 2, 1 - lat % 2]
+    targets = [{name: jnp.where(way == 1, up[name], down[name]) for name in up} for way in upward]
+    slots = [
+        jnp.where(way == 1, jnp.where(lat < lat_count - 1, 0, 1), jnp.where(lat > 0, 1, 0)) for way in upward
+    ]
+    for target in targets:
+        pl.semaphore_signal(barrier, inc=1, device_id=target, device_id_type=MESH)
 
     for scalar in scalars:
         scalar.wait()
     first = lat * rows
     cuts = column(cuts_ref, first, jnp.int32)
     on = jnp.where(column(flags_ref, first, jnp.int32) > 0, 1.0, 0.0)
-    merid = column(merid_ref, first)
+    at_end = jnp.where(lat == 0, 0, jnp.where(lat == lat_count - 1, rows - 1, -1))
+    row = lax.broadcasted_iota(jnp.int32, (rows, LANES), 0)
+    brink = jnp.where(row == at_end, 0.0, column(merid_ref, first))
     kept = (2 * cuts + 1).astype(jnp.float32)
     keep = jnp.where(on > 0.0, kept * (1.0 / circle), 1.0)
     odd = jnp.bitwise_and(cuts, 1)
@@ -313,16 +324,15 @@
     def spread(value):
         return jnp.broadcast_to(value[None], (levels,) + value.shape).reshape(count, value.shape[1])
 
-    def climb(which):
+    groups = cells // TILE // GROUP
+
+    def send(turn, which, group, slot):
+        at = pl.ds(group * GROUP * TILE, GROUP * TILE)
+        place = which * groups + group
         return pltpu.make_async_remote_copy(
-            src_ref=brink_ref.at[1, which], dst_ref=edges_ref.at[0, which], send_sem=up_sem.at[which],
-            recv_sem=up_in_sem.at[which], device_id={"lat": lat + 1}, device_id_type=MESH,
-        )
-
-    def descend(which):
-        return pltpu.make_async_remote_copy(
-            src_ref=brink_ref.at[0, which], dst_ref=edges_ref.at[1, which], send_sem=down_sem.at[which],
-            recv_sem=down_in_sem.at[which], device_id={"lat": lat - 1}, device_id_type=MESH,
+            src_ref=brink_ref.at[upward[turn], which, :, at], dst_ref=edges_ref.at[slot, which, :, at],
+            send_sem=leave_sem.at[turn, place], recv_sem=reach_sem.at[slot, place],
+            device_id=targets[turn], device_id_type=MESH,
         )
 
     lane_all = lax.broadcasted_iota(jnp.int32, (count, LANES), 1)
@@ -360,17 +370,8 @@
             message = jnp.where(lane_all == OWN + 32, end, jnp.where(lane_all == OWN + 33, start, message))
         send_ref[field] = jnp.where(lane_all[:half] < 64, message[:half], pltpu.roll(message[half:], 64, 1))
         if turn == 0:
-            greeted = 1 + jnp.where(lat > 0, 1, 0) + jnp.where(lat < lat_count - 1, 1, 0)
-            pl.semaphore_wait(barrier, greeted)
+            pl.semaphore_wait(barrier, 3)
         exchange(field).start()
-
-    @pl.when(lat == 0)
-    def _():
-        edges_ref[0] = jnp.zeros(edges_ref.shape[1:], jnp.float32)
-
-    @pl.when(lat == lat_count - 1)
-    def _():
-        edges_ref[1] = jnp.zeros(edges_ref.shape[1:], jnp.float32)
 
     tables[2].wait()
     tables[3].wait()
@@ -383,6 +384,9 @@
             rims = taken + pltpu.roll(edge_ref[field], LANES - 2, 1)
             if field == 0:
                 rims = rims * turned
+            rims = jnp.where(
+                lane_all == LANES - 1, pltpu.roll(rims, LANES - 2 - OWN, 1), pltpu.roll(rims, LANES - OWN, 1)
+            )
             rims_ref[field] = rims.reshape(levels, rows, LANES)
         signs = spread(sign)
         code = code_ref[field]
@@ -392,11 +396,20 @@
                 jnp.where(lane_all < REMOTE, -signs * taken, code[count:]),
             ]
         )
-        code_high, code_low = halves(code)
+        code_high = code.astype(jnp.bfloat16).astype(jnp.float32)
+        code_low = code - code_high
+        lane_both = lax.broadcasted_iota(jnp.int32, code.shape, 1)
+        packed = []
+        for low, head, rest in (
+            (pltpu.roll(code_low, CODES, 1), code_high, pltpu.roll(code_high, 32, 1)),
+            (code_low, pltpu.roll(code_high, 48, 1), pltpu.roll(code_high, 80, 1)),
+        ):
+            pair = (jnp.where(lane_both < CODES, head, low), jnp.where(lane_both < 32, low, rest))
+            packed.append([value.astype(jnp.bfloat16) for value in pair])
         for block in range(cells // TILE):
             at = slice(block * TILE, (block + 1) * TILE)
             high, low = high_ref[field, :, at], low_ref[field, :, at]
-            terms = jnp.concatenate([high, low, high, code_high, code_low, code_high], axis=1)
+            terms = jnp.concatenate([high, low, high, *packed[2 * at.start // cells]], axis=1)
             weights = jnp.concatenate([near_ref[...], expand_ref[:, at]], axis=0)
             value = jnp.dot(terms, weights, preferred_element_type=jnp.float32)
             shape = (levels, rows, TILE)
@@ -408,35 +421,22 @@
                 edge = result
                 if field == 0:
                     edge = result * depth_ref[:, :, at].astype(jnp.float32)
-                edge = edge * across(merid, TILE)[None]
+                edge = edge * across(brink, TILE)[None]
                 which = 0 if field == 2 else 1
                 brink_ref[0, which, :, at] = edge[:, 0, :]
                 brink_ref[1, which, :, at] = edge[:, rows - 1, :]
-        if field != 1:
-            which = 0 if field == 2 else 1
-
-            @pl.when(lat < lat_count - 1)
-            def _():
-                climb(which).start()
-
-            @pl.when(lat > 0)
-            def _():
-                descend(which).start()
+                if block % GROUP == GROUP - 1:
+                    for turn in range(2):
+                        send(turn, which, block // GROUP, slots[turn]).start()
 
     for field in ORDER:
         exchange(field).wait_send()
 
-    @pl.when(lat < lat_count - 1)
-    def _():
-        for which in range(2):
-            climb(which).wait_send()
-            descend(which).wait_recv()
-
-    @pl.when(lat > 0)
-    def _():
-        for which in range(2):
-            descend(which).wait_send()
-            climb(which).wait_recv()
+    for which in range(2):
+        for group in range(groups):
+            for turn in range(2):
+                send(turn, which, group, slots[turn]).wait_send()
+                send(turn, which, group, turn).wait_recv()
 
 
 def final_kernel(
@@ -449,11 +449,13 @@
     merid = across(column(merid_ref, first), cells)
     coriolis = across(column(coriolis_ref, first), cells)
     row = lax.broadcasted_iota(jnp.int32, (rows, cells), 0)
-    lane = lax.broadcasted_iota(jnp.int32, (rows, cells), 1)
-
-    def zonal_adjoint(value, west, east):
-        left = jnp.where(lane == 0, west, pltpu.roll(value, 1, 1))
-        right = jnp.where(lane == cells - 1, east, pltpu.roll(value, cells - 1, 1))
+    lane = lax.broadcasted_iota(jnp.int32, (rows, LANES), 1)
+
+    def zonal_adjoint(value, rims):
+        left, right = pltpu.roll(value, 1, 1), pltpu.roll(value, cells - 1, 1)
+        left = jnp.concatenate([jnp.where(lane == 0, rims, left[:, :LANES]), left[:, LANES:]], axis=1)
+        split = cells - LANES
+        right = jnp.concatenate([right[:, :split], jnp.where(lane == LANES - 1, rims, right[:, split:])], axis=1)
         return zonal * (left - right)
 
     def merid_adjoint(value, before, after):
@@ -474,13 +476,13 @@
         line = pl.ds(level, 1)
         flux_rims, east_rims = rims_ref[0, level], rims_ref[1, level]
         run = run - (
-            zonal_adjoint(east, east_rims[:, OWN : OWN + 1], east_rims[:, OWN + 1 : OWN + 2])
+            zonal_adjoint(east, east_rims)
             + merid_adjoint(north, edges_ref[0, 0, line, :], edges_ref[1, 0, line, :])
         )
         out_ref[0, turn] = x_ref[0, level] + weight_ref[level] * run
         out_ref[1, turn] = (
             x_ref[1, level]
-            - zonal_adjoint(flux, flux_rims[:, OWN : OWN + 1], flux_rims[:, OWN + 1 : OWN + 2])
+            - zonal_adjoint(flux, flux_rims)
             - coriolis * north
         )
         out_ref[2, turn] = (
@@ -495,27 +497,28 @@
     fields, level_count, rows, cells = adjoint.shape
     project, expand, near = (jnp.asarray(table) for table in kernel_tables(cells))
     count = level_count * rows
+    pieces = cells // TILE // GROUP
     scalars = pl.BlockSpec(memory_space=pltpu.SMEM)
     there = pl.BlockSpec(memory_space=pltpu.HBM)
     close = pl.BlockSpec(memory_space=pltpu.VMEM)
     single = jnp.float32
     dma = pltpu.SemaphoreType.DMA
 
-    q, rims, edges = pl.pallas_call(
+    q, rims, edges, adjoint_near, depth_near = pl.pallas_call(
         filter_kernel,
         in_specs=[there] * 8,
-        out_specs=[close] * 3,
+        out_specs=[close] * 5,
         out_shape=[
             jax.ShapeDtypeStruct(adjoint.shape, single),
             jax.ShapeDtypeStruct((2, level_count, rows, LANES), single),
             jax.ShapeDtypeStruct((2, 2, level_count, cells), single),
+            jax.ShapeDtypeStruct(adjoint.shape, single),
+            jax.ShapeDtypeStruct(depth.shape, depth.dtype),
         ],
         scratch_shapes=[
             pltpu.SMEM(merid_coef.shape, single),
             pltpu.SMEM(cutoffs.shape, jnp.int32),
             pltpu.SMEM(polar_flags.shape, jnp.int32),
-            pltpu.VMEM(adjoint.shape, single),
-            pltpu.VMEM(depth.shape, depth.dtype),
             pltpu.VMEM(project.shape, project.dtype),
             pltpu.VMEM(expand.shape, expand.dtype),
             pltpu.VMEM(near.shape, near.dtype),
@@ -532,10 +535,8 @@
             dma((4,)),
             dma((3,)),
             dma((3,)),
-            dma((2,)),
-            dma((2,)),
-            dma((2,)),
-            dma((2,)),
+            dma((2, 2 * pieces)),
+            dma((2, 2 * pieces)),
         ],
         compiler_params=pltpu.CompilerParams(
             collective_id=0, has_side_effects=True, vmem_limit_bytes=36 * 2**20
@@ -552,7 +553,7 @@
         out_shape=jax.ShapeDtypeStruct(adjoint.shape, single),
         scratch_shapes=[pltpu.VMEM((rows, cells), single)],
         compiler_params=pltpu.CompilerParams(vmem_limit_bytes=32 * 2**20),
-    )(zonal_coef, merid_coef, coriolis, layer_weight, adjoint, q, depth, edges, rims)
+    )(zonal_coef, merid_coef, coriolis, layer_weight, adjoint_near, q, depth_near, edges, rims)
 
 
 def plan_for(mesh):

time: 24.4 us -> 23.2 us (0.951)
  the two profiles are of different devices: /device:TPU:1 before, /device:TPU:0 now
where the time goes in v3:
time: 23.2 us; the launch traced here: 23.1 us
  Pallas kernels  23 us (99%)
    pallas_call x1, Pallas kernels, on_pair(): pl.pallas_call(filter_kernel, in_specs=[there] * 8, out_specs=[close] * 5...  18.7 us
    pallas_call x1, Pallas kernels, on_pair(): pl.pallas_call(final_kernel, grid=(level_count // part,), in_specs=[scala...  4.28 us

profile of v3, /device:TPU:0, one launch (start us, length us, event | category | flops | bytes accessed | tf_op | source)
XLA Modules:
  0.0 23.1 jit_solution(2733555283244099799)
XLA Ops:
  0.0 0.0 copy-start
  0.0 0.0 copy-start.3
  0.0 0.0 copy-start.2
  0.0 0.0 copy-start.1
  0.0 18.7 %shard_map.109 = (f32[3,32,8,1536]{3,2,1,0:T(8,128)S(1)}, f32[2,32,8,128]{3,2,1,0:T(8,128)S(1)}, f32[2,2,32,1536]{3,2,1,0:T(8,128)S(1)}, f32[3,32,8,1536]{3,2,1,0:T(8,128)S(1)}, bf16[32,8,1536]{2,1,0:T(8,128)(2,1)S(1)}) custom-call(f32[64]{0:T(128)} %merid_ref.1, s32[64]{0:T(128)} %cuts_hbm.1, s32[64]{0:T(128)} %flags_hbm.1, f32[3,32,8,1536]{3,2,1,0:T(8,128)} %x_hbm.1, ...), custom_call_target="tpu_custom_call" | custom-call | tf_op jit(solution)/shard_map/pallas_call | solution.py:507
  18.7 0.0 copy-done
  18.7 0.0 copy-done.3
  18.8 0.0 copy-done.2
  18.8 0.0 copy-done.1
  18.8 4.3 %shard_map.110 = f32[3,32,8,1536]{3,2,1,0:T(8,128)} custom-call(f32[64]{0:T(128)S(1)} %copy-done.1, f32[64]{0:T(128)S(1)} %copy-done, f32[64]{0:T(128)S(1)} %copy-done.2, f32[32]{0:T(128)S(1)} %copy-done.3, f32[3,32,8,1536]{3,2,1,0:T(8,128)S(1)} %get-tuple-element.10.x_ref, f32[3,32,8,1536]{3,2,1,0:T(8,128)S(1)} %get-tuple-element.11.q_ref, ...), custom_call_target="tpu_custom_call" | custom-call | tf_op jit(solution)/shard_map/pallas_call | solution.py:548
Async XLA Ops:
  0.0 18.7 %copy-start = (f32[64]{0:T(128)S(1)}, f32[64]{0:T(128)}, u32[]{:S(2)}) copy-start(f32[64]{0:T(128)} %merid_ref.1) | copy-start | bytes 772
  0.0 18.7 %copy-start.3 = (f32[32]{0:T(128)S(1)}, f32[32]{0:T(128)}, u32[]{:S(2)}) copy-start(f32[32]{0:T(128)} %weight_ref.1) | copy-start | bytes 388
  0.0 18.7 %copy-start.2 = (f32[64]{0:T(128)S(1)}, f32[64]{0:T(128)}, u32[]{:S(2)}) copy-start(f32[64]{0:T(128)} %coriolis_ref.1) | copy-start | bytes 772
  0.0 18.8 %copy-start.1 = (f32[64]{0:T(128)S(1)}, f32[64]{0:T(128)}, u32[]{:S(2)}) copy-start(f32[64]{0:T(128)} %zonal_ref.1) | copy-start | bytes 772

commit v4 on v3

--- a/solution.py
+++ b/solution.py
@@ -153,6 +153,7 @@
 OTHER = 30
 FAR = 32
 CODES = 80
+PART = 8
 GROUP = 2
 TILE = 256
 LANES = 128
@@ -237,9 +238,10 @@
 
 
 def filter_kernel(
-    merid_hbm, cuts_hbm, flags_hbm, x_hbm, depth_hbm, project_hbm, expand_hbm, near_hbm,
-    q_ref, rims_ref, edges_ref, x_ref, depth_ref,
-    merid_ref, cuts_ref, flags_ref, project_ref, expand_ref, near_ref, high_ref, low_ref, code_ref, edge_ref, send_ref, take_ref,
+    merid_hbm, cuts_hbm, flags_hbm, zonal_hbm, coriolis_hbm, weight_hbm, x_hbm, depth_hbm, project_hbm, expand_hbm, near_hbm,
+    out_ref, edges_ref,
+    merid_ref, cuts_ref, flags_ref, zonal_ref, coriolis_ref, weight_ref, q_ref, rims_ref, x_ref, depth_ref,
+    project_ref, expand_ref, near_ref, high_ref, low_ref, code_ref, edge_ref, send_ref, take_ref,
     rows_ref, brink_ref, scalar_sem, load_sem, table_sem, out_sem, in_sem, leave_sem, reach_sem,
 ):
     fields, levels, rows, cells = x_ref.shape
@@ -252,7 +254,10 @@
     scalars = [
         pltpu.make_async_copy(source, target, scalar_sem.at[turn])
         for turn, (source, target) in enumerate(
-            ((cuts_hbm, cuts_ref), (flags_hbm, flags_ref), (merid_hbm, merid_ref))
+            (
+                (cuts_hbm, cuts_ref), (flags_hbm, flags_ref), (merid_hbm, merid_ref),
+                (zonal_hbm, zonal_ref), (coriolis_hbm, coriolis_ref), (weight_hbm, weight_ref),
+            )
         )
     ]
     for scalar in scalars:
@@ -292,7 +297,10 @@
     on = jnp.where(column(flags_ref, first, jnp.int32) > 0, 1.0, 0.0)
     at_end = jnp.where(lat == 0, 0, jnp.where(lat == lat_count - 1, rows - 1, -1))
     row = lax.broadcasted_iota(jnp.int32, (rows, LANES), 0)
-    brink = jnp.where(row == at_end, 0.0, column(merid_ref, first))
+    merid = column(merid_ref, first)
+    zonal = column(zonal_ref, first)
+    coriolis = column(coriolis_ref, first)
+    brink = jnp.where(row == at_end, 0.0, merid)
     kept = (2 * cuts + 1).astype(jnp.float32)
     keep = jnp.where(on > 0.0, kept * (1.0 / circle), 1.0)
     odd = jnp.bitwise_and(cuts, 1)
@@ -375,6 +383,35 @@
 
     tables[2].wait()
     tables[3].wait()
+    lane_row = lax.broadcasted_iota(jnp.int32, (rows, LANES), 1)
+    row_all = lax.broadcasted_iota(jnp.int32, (rows, cells), 0)
+
+    def zonal_adjoint(value, rims):
+        left, right = pltpu.roll(value, 1, 1), pltpu.roll(value, cells - 1, 1)
+        left = jnp.concatenate([jnp.where(lane_row == 0, rims, left[:, :LANES]), left[:, LANES:]], axis=1)
+        last = cells - LANES
+        right = jnp.concatenate([right[:, :last], jnp.where(lane_row == LANES - 1, rims, right[:, last:])], axis=1)
+        return across(zonal, cells) * (left - right)
+
+    def merid_adjoint(value):
+        value = across(merid, cells) * value
+        up = jnp.where(row_all == 0, 0.0, pltpu.roll(value, 1, 0))
+        down = jnp.where(row_all == rows - 1, 0.0, pltpu.roll(value, rows - 1, 0))
+        return up - down
+
+    def fluxes(level):
+        north = q_ref[2, level]
+        flux = depth_ref[level].astype(jnp.float32) * q_ref[0, level]
+        out_ref[1, level] = x_ref[1, level] - zonal_adjoint(flux, rims_ref[0, level]) - across(coriolis, cells) * north
+        out_ref[2, level] = x_ref[2, level] - merid_adjoint(flux)
+
+    def forces(level, run):
+        east = q_ref[1, level]
+        run = run - (zonal_adjoint(east, rims_ref[1, level]) + out_ref[0, level])
+        out_ref[0, level] = x_ref[0, level] + weight_ref[level] * run
+        out_ref[2, level] += across(coriolis, cells) * east
+        return run
+
     for field in ORDER:
         exchange(field).wait_recv()
         taken = take_ref[field]
@@ -417,6 +454,11 @@
             result = result + rows_ref[1, :, at][None] * value[:count].reshape(shape)
             result = result - rows_ref[0, :, at][None] * value[count:].reshape(shape)
             q_ref[field, :, :, at] = result
+            turns = range(block * levels * TILE // cells, (block + 1) * levels * TILE // cells)
+            for level in turns if field == 0 else ():
+                out_ref[0, level] = merid_adjoint(q_ref[2, level])
+            for level in turns if field == 1 else ():
+                fluxes(level)
             if field != 1:
                 edge = result
                 if field == 0:
@@ -429,6 +471,13 @@
                     for turn in range(2):
                         send(turn, which, block // GROUP, slots[turn]).start()
 
+    def tail(step, run):
+        for turn in range(4):
+            level = step * 4 + turn
+            run = forces(level, run)
+        return run
+
+    lax.fori_loop(0, levels // 4, tail, jnp.zeros((rows, cells), jnp.float32))
     for field in ORDER:
         exchange(field).wait_send()
 
@@ -439,58 +488,30 @@
                 send(turn, which, group, turn).wait_recv()
 
 
-def final_kernel(
-    zonal_ref, merid_ref, coriolis_ref, weight_ref, x_ref, q_ref, depth_ref, edges_ref, rims_ref, out_ref, run_ref
-):
-    step = pl.program_id(0)
-    _, levels, rows, cells = out_ref.shape
-    first = lax.axis_index("lat") * rows
-    zonal = across(column(zonal_ref, first), cells)
-    merid = across(column(merid_ref, first), cells)
-    coriolis = across(column(coriolis_ref, first), cells)
+def final_kernel(weight_ref, part_ref, edges_ref, out_hbm, done_ref, sems):
+    _, levels, rows, cells = part_ref.shape
     row = lax.broadcasted_iota(jnp.int32, (rows, cells), 0)
-    lane = lax.broadcasted_iota(jnp.int32, (rows, LANES), 1)
-
-    def zonal_adjoint(value, rims):
-        left, right = pltpu.roll(value, 1, 1), pltpu.roll(value, cells - 1, 1)
-        left = jnp.concatenate([jnp.where(lane == 0, rims, left[:, :LANES]), left[:, LANES:]], axis=1)
-        split = cells - LANES
-        right = jnp.concatenate([right[:, :split], jnp.where(lane == LANES - 1, rims, right[:, split:])], axis=1)
-        return zonal * (left - right)
-
-    def merid_adjoint(value, before, after):
-        value = merid * value
-        up = jnp.where(row == 0, before, pltpu.roll(value, 1, 0))
-        down = jnp.where(row == rows - 1, after, pltpu.roll(value, rows - 1, 0))
-        return up - down
-
-    @pl.when(step == 0)
-    def _():
-        run_ref[...] = jnp.zeros_like(run_ref)
-
-    run = run_ref[...]
-    for turn in range(levels):
-        level = step * levels + turn
-        height, east, north = q_ref[0, level], q_ref[1, level], q_ref[2, level]
-        flux = depth_ref[level].astype(jnp.float32) * height
-        line = pl.ds(level, 1)
-        flux_rims, east_rims = rims_ref[0, level], rims_ref[1, level]
-        run = run - (
-            zonal_adjoint(east, east_rims)
-            + merid_adjoint(north, edges_ref[0, 0, line, :], edges_ref[1, 0, line, :])
-        )
-        out_ref[0, turn] = x_ref[0, level] + weight_ref[level] * run
-        out_ref[1, turn] = (
-            x_ref[1, level]
-            - zonal_adjoint(flux, flux_rims)
-            - coriolis * north
-        )
-        out_ref[2, turn] = (
-            x_ref[2, level]
-            - merid_adjoint(flux, edges_ref[0, 1, line, :], edges_ref[1, 1, line, :])
-            + coriolis * east
-        )
-    run_ref[...] = run
+    copies = [pltpu.make_async_copy(part_ref.at[1], out_hbm.at[1], sems.at[0])]
+    copies[0].start()
+
+    def missing(which, level):
+        before, after = edges_ref[0, which, level : level + 1, :], edges_ref[1, which, level : level + 1, :]
+        return jnp.where(row == 0, before, jnp.where(row == rows - 1, -after, 0.0))
+
+    run = jnp.zeros((rows, cells), jnp.float32)
+    for level in range(levels):
+        run = run - missing(0, level)
+        done_ref[0, level] = part_ref[0, level] + weight_ref[level] * run
+        done_ref[1, level] = part_ref[2, level] - missing(1, level)
+        if level % PART == PART - 1:
+            at = pl.ds(level - PART + 1, PART)
+            for turn, field in enumerate((0, 2)):
+                copies.append(
+                    pltpu.make_async_copy(done_ref.at[turn, at], out_hbm.at[field, at], sems.at[len(copies)])
+                )
+                copies[-1].start()
+    for copy in copies:
+        copy.wait()
 
 
 def on_pair(adjoint, depth, zonal_coef, merid_coef, coriolis, layer_weight, cutoffs, polar_flags):
@@ -504,21 +525,25 @@
     single = jnp.float32
     dma = pltpu.SemaphoreType.DMA
 
-    q, rims, edges, adjoint_near, depth_near = pl.pallas_call(
+    partial, edges = pl.pallas_call(
         filter_kernel,
-        in_specs=[there] * 8,
-        out_specs=[close] * 5,
+        in_specs=[there] * 11,
+        out_specs=[close] * 2,
         out_shape=[
             jax.ShapeDtypeStruct(adjoint.shape, single),
-            jax.ShapeDtypeStruct((2, level_count, rows, LANES), single),
             jax.ShapeDtypeStruct((2, 2, level_count, cells), single),
-            jax.ShapeDtypeStruct(adjoint.shape, single),
-            jax.ShapeDtypeStruct(depth.shape, depth.dtype),
         ],
         scratch_shapes=[
             pltpu.SMEM(merid_coef.shape, single),
             pltpu.SMEM(cutoffs.shape, jnp.int32),
             pltpu.SMEM(polar_flags.shape, jnp.int32),
+            pltpu.SMEM(zonal_coef.shape, single),
+            pltpu.SMEM(coriolis.shape, single),
+            pltpu.SMEM(layer_weight.shape, single),
+            pltpu.VMEM(adjoint.shape, single),
+            pltpu.VMEM((2, level_count, rows, LANES), single),
+            pltpu.VMEM(adjoint.shape, single),
+            pltpu.VMEM(depth.shape, depth.dtype),
             pltpu.VMEM(project.shape, project.dtype),
             pltpu.VMEM(expand.shape, expand.dtype),
             pltpu.VMEM(near.shape, near.dtype),
@@ -530,7 +555,7 @@
             pltpu.VMEM((fields, count // 2, LANES), single),
             pltpu.VMEM((2, rows, cells), single),
             pltpu.VMEM((2, 2, level_count, cells), single),
-            dma((3,)),
+            dma((6,)),
             dma((3,)),
             dma((4,)),
             dma((3,)),
@@ -541,19 +566,16 @@
         compiler_params=pltpu.CompilerParams(
             collective_id=0, has_side_effects=True, vmem_limit_bytes=36 * 2**20
         ),
-    )(*(pltpu.with_memory_space_constraint(value, pltpu.HBM) for value in (merid_coef, cutoffs, polar_flags, adjoint, depth, project, expand, near)))
-
-    part = 8
-    four = pl.BlockSpec((fields, part, rows, cells), lambda i: (0, i, 0, 0))
+    )(*(pltpu.with_memory_space_constraint(value, pltpu.HBM) for value in (merid_coef, cutoffs, polar_flags, zonal_coef, coriolis, layer_weight, adjoint, depth, project, expand, near)))
+
     return pl.pallas_call(
         final_kernel,
-        grid=(level_count // part,),
-        in_specs=[scalars] * 4 + [close] * 5,
-        out_specs=four,
+        in_specs=[scalars] + [close] * 2,
+        out_specs=pl.BlockSpec(memory_space=pl.ANY),
         out_shape=jax.ShapeDtypeStruct(adjoint.shape, single),
-        scratch_shapes=[pltpu.VMEM((rows, cells), single)],
+        scratch_shapes=[pltpu.VMEM((2,) + adjoint.shape[1:], single), dma((1 + 2 * level_count // PART,))],
         compiler_params=pltpu.CompilerParams(vmem_limit_bytes=32 * 2**20),
-    )(zonal_coef, merid_coef, coriolis, layer_weight, adjoint_near, q, depth_near, edges, rims)
+    )(layer_weight, partial, edges)
 
 
 def plan_for(mesh):

time: 23.2 us -> 21.7 us (0.935)
  Pallas kernels: 23 us -> 21.6 us
    pallas_call x2, Pallas kernels: 23 us -> 21.6 us  [the longest x1 18.8 us: on_pair(): pl.pallas_call(filter_kernel, in_specs=[there] * 11, out_specs=[close] *...]
where the time goes in v4:
time: 21.7 us; the launch traced here: 21.6 us
  Pallas kernels  21.6 us (100%)
    pallas_call x1, Pallas kernels, on_pair(): pl.pallas_call(filter_kernel, in_specs=[there] * 11, out_specs=[close] *...  18.8 us
    pallas_call x1, Pallas kernels, on_pair(): pl.pallas_call(final_kernel, in_specs=[scalars] + [close] * 2, out_specs=...  2.79 us

profile of v4, /device:TPU:0, one launch (start us, length us, event | category | flops | bytes accessed | tf_op | source)
XLA Modules:
  0.0 21.6 jit_solution(13584728205750729157)
XLA Ops:
  0.0 0.0 copy-start
  0.0 18.8 %shard_map.109 = (f32[3,32,8,1536]{3,2,1,0:T(8,128)S(1)}, f32[2,2,32,1536]{3,2,1,0:T(8,128)S(1)}) custom-call(f32[64]{0:T(128)} %merid_hbm.1, s32[64]{0:T(128)} %cuts_hbm.1, s32[64]{0:T(128)} %flags_hbm.1, f32[64]{0:T(128)} %zonal_hbm.1, f32[64]{0:T(128)} %coriolis_hbm.1, f32[32]{0:T(128)} %weight_ref.1, f32[3,32,8,1536]{3,2,1,0:T(8,128)} %x_hbm.1, ...), custom_call_target="tpu_custom_call" | custom-call | tf_op jit(solution)/shard_map/pallas_call | solution.py:528
  18.8 0.0 copy-done
  18.8 2.8 %shard_map.110 = f32[3,32,8,1536]{3,2,1,0:T(8,128)} custom-call(f32[32]{0:T(128)S(1)} %copy-done, f32[3,32,8,1536]{3,2,1,0:T(8,128)S(1)} %get-tuple-element.7.part_ref, f32[2,2,32,1536]{3,2,1,0:T(8,128)S(1)} %get-tuple-element.8.edges_ref), custom_call_target="tpu_custom_call" | custom-call | tf_op jit(solution)/shard_map/pallas_call | solution.py:571
Async XLA Ops:
  0.0 18.8 %copy-start = (f32[32]{0:T(128)S(1)}, f32[32]{0:T(128)}, u32[]{:S(2)}) copy-start(f32[32]{0:T(128)} %weight_ref.1) | copy-start | bytes 388

commit v5 on v4

--- a/solution.py
+++ b/solution.py
@@ -262,14 +262,21 @@
     ]
     for scalar in scalars:
         scalar.start()
-    loads = [pltpu.make_async_copy(x_hbm.at[f], x_ref.at[f], load_sem.at[f]) for f in range(fields)]
+    loads = {f: pltpu.make_async_copy(x_hbm.at[f], x_ref.at[f], load_sem.at[f]) for f in ORDER[1:]}
+    quarters = [
+        pltpu.make_async_copy(
+            x_hbm.at[ORDER[0], pl.ds(start, 8)], x_ref.at[ORDER[0], pl.ds(start, 8)], load_sem.at[fields + start // 8]
+        )
+        for start in range(0, levels, 8)
+    ]
     tables = [
         pltpu.make_async_copy(source, target, table_sem.at[turn])
         for turn, (source, target) in enumerate(
             ((project_hbm, project_ref), (depth_hbm, depth_ref), (near_hbm, near_ref), (expand_hbm, expand_ref))
         )
     ]
-    loads[ORDER[0]].start()
+    for quarter in quarters:
+        quarter.start()
     tables[0].start()
     loads[ORDER[1]].start()
     tables[1].start()
@@ -346,8 +353,11 @@
     lane_all = lax.broadcasted_iota(jnp.int32, (count, LANES), 1)
     part = 8
     for turn, field in enumerate(ORDER):
-        loads[field].wait()
+        if field != ORDER[0]:
+            loads[field].wait()
         for group in range(levels // part):
+            if field == ORDER[0]:
+                quarters[group].wait()
             x = x_ref[field, group * part : (group + 1) * part]
             for which in range(2):
                 high, low = halves((x * rows_ref[which][None]).reshape(part * rows, cells))
@@ -407,7 +417,7 @@
 
     def forces(level, run):
         east = q_ref[1, level]
-        run = run - (zonal_adjoint(east, rims_ref[1, level]) + out_ref[0, level])
+        run = run - (zonal_adjoint(east, rims_ref[1, level]) + merid_adjoint(q_ref[2, level]))
         out_ref[0, level] = x_ref[0, level] + weight_ref[level] * run
         out_ref[2, level] += across(coriolis, cells) * east
         return run
@@ -455,8 +465,6 @@
             result = result - rows_ref[0, :, at][None] * value[count:].reshape(shape)
             q_ref[field, :, :, at] = result
             turns = range(block * levels * TILE // cells, (block + 1) * levels * TILE // cells)
-            for level in turns if field == 0 else ():
-                out_ref[0, level] = merid_adjoint(q_ref[2, level])
             for level in turns if field == 1 else ():
                 fluxes(level)
             if field != 1:
@@ -556,7 +564,7 @@
             pltpu.VMEM((2, rows, cells), single),
             pltpu.VMEM((2, 2, level_count, cells), single),
             dma((6,)),
-            dma((3,)),
+            dma((3 + level_count // 8,)),
             dma((4,)),
             dma((3,)),
             dma((3,)),

time: 21.7 us -> 21.1 us (0.972)
  Pallas kernels: 21.6 us -> 21 us
    pallas_call x1, Pallas kernels: 18.8 us -> 18.2 us  [on_pair(): pl.pallas_call(filter_kernel, in_specs=[there] * 11, out_specs=[close] *...]
where the time goes in v5:
time: 21.1 us; the launch traced here: 21 us
  Pallas kernels  21 us (100%)
    pallas_call x1, Pallas kernels, on_pair(): pl.pallas_call(filter_kernel, in_specs=[there] * 11, out_specs=[close] *...  18.2 us
    pallas_call x1, Pallas kernels, on_pair(): pl.pallas_call(final_kernel, in_specs=[scalars] + [close] * 2, out_specs=...  2.79 us

profile of v5, /device:TPU:0, one launch (start us, length us, event | category | flops | bytes accessed | tf_op | source)
XLA Modules:
  0.0 21.0 jit_solution(17490081151280268381)
XLA Ops:
  0.0 0.0 copy-start
  0.0 18.2 %shard_map.109 = (f32[3,32,8,1536]{3,2,1,0:T(8,128)S(1)}, f32[2,2,32,1536]{3,2,1,0:T(8,128)S(1)}) custom-call(f32[64]{0:T(128)} %merid_hbm.1, s32[64]{0:T(128)} %cuts_hbm.1, s32[64]{0:T(128)} %flags_hbm.1, f32[64]{0:T(128)} %zonal_hbm.1, f32[64]{0:T(128)} %coriolis_hbm.1, f32[32]{0:T(128)} %weight_ref.1, f32[3,32,8,1536]{3,2,1,0:T(8,128)} %x_hbm.1, ...), custom_call_target="tpu_custom_call" | custom-call | tf_op jit(solution)/shard_map/pallas_call | solution.py:536
  18.2 0.0 copy-done
  18.2 2.8 %shard_map.110 = f32[3,32,8,1536]{3,2,1,0:T(8,128)} custom-call(f32[32]{0:T(128)S(1)} %copy-done, f32[3,32,8,1536]{3,2,1,0:T(8,128)S(1)} %get-tuple-element.7.part_ref, f32[2,2,32,1536]{3,2,1,0:T(8,128)S(1)} %get-tuple-element.8.edges_ref), custom_call_target="tpu_custom_call" | custom-call | tf_op jit(solution)/shard_map/pallas_call | solution.py:579
Async XLA Ops:
  0.0 18.2 %copy-start = (f32[32]{0:T(128)S(1)}, f32[32]{0:T(128)}, u32[]{:S(2)}) copy-start(f32[32]{0:T(128)} %weight_ref.1) | copy-start | bytes 388

commit v6 on v5

--- a/solution.py
+++ b/solution.py
@@ -480,12 +480,12 @@
                         send(turn, which, block // GROUP, slots[turn]).start()
 
     def tail(step, run):
-        for turn in range(4):
-            level = step * 4 + turn
+        for turn in range(8):
+            level = step * 8 + turn
             run = forces(level, run)
         return run
 
-    lax.fori_loop(0, levels // 4, tail, jnp.zeros((rows, cells), jnp.float32))
+    lax.fori_loop(0, levels // 8, tail, jnp.zeros((rows, cells), jnp.float32))
     for field in ORDER:
         exchange(field).wait_send()
 

time: 21.1 us -> 21.1 us (level)
  no operation moved by 1% of the time
where the time goes in v6:
time: 21.1 us; the launch traced here: 21 us
  Pallas kernels  21 us (100%)
    pallas_call x1, Pallas kernels, on_pair(): pl.pallas_call(filter_kernel, in_specs=[there] * 11, out_specs=[close] *...  18.2 us
    pallas_call x1, Pallas kernels, on_pair(): pl.pallas_call(final_kernel, in_specs=[scalars] + [close] * 2, out_specs=...  2.79 us

profile of v6, /device:TPU:0, one launch (start us, length us, event | category | flops | bytes accessed | tf_op | source)
XLA Modules:
  0.0 21.0 jit_solution(15890858018918286135)
XLA Ops:
  0.0 0.0 copy-start
  0.0 18.2 %shard_map.109 = (f32[3,32,8,1536]{3,2,1,0:T(8,128)S(1)}, f32[2,2,32,1536]{3,2,1,0:T(8,128)S(1)}) custom-call(f32[64]{0:T(128)} %merid_hbm.1, s32[64]{0:T(128)} %cuts_hbm.1, s32[64]{0:T(128)} %flags_hbm.1, f32[64]{0:T(128)} %zonal_hbm.1, f32[64]{0:T(128)} %coriolis_hbm.1, f32[32]{0:T(128)} %weight_ref.1, f32[3,32,8,1536]{3,2,1,0:T(8,128)} %x_hbm.1, ...), custom_call_target="tpu_custom_call" | custom-call | tf_op jit(solution)/shard_map/pallas_call | solution.py:536
  18.2 0.0 copy-done
  18.2 2.8 %shard_map.110 = f32[3,32,8,1536]{3,2,1,0:T(8,128)} custom-call(f32[32]{0:T(128)S(1)} %copy-done, f32[3,32,8,1536]{3,2,1,0:T(8,128)S(1)} %get-tuple-element.7.part_ref, f32[2,2,32,1536]{3,2,1,0:T(8,128)S(1)} %get-tuple-element.8.edges_ref), custom_call_target="tpu_custom_call" | custom-call | tf_op jit(solution)/shard_map/pallas_call | solution.py:579
Async XLA Ops:
  0.0 18.2 %copy-start = (f32[32]{0:T(128)S(1)}, f32[32]{0:T(128)}, u32[]{:S(2)}) copy-start(f32[32]{0:T(128)} %weight_ref.1) | copy-start | bytes 388

commit v7 on v6

--- a/solution.py
+++ b/solution.py
@@ -480,12 +480,12 @@
                         send(turn, which, block // GROUP, slots[turn]).start()
 
     def tail(step, run):
-        for turn in range(8):
-            level = step * 8 + turn
+        for turn in range(16):
+            level = step * 16 + turn
             run = forces(level, run)
         return run
 
-    lax.fori_loop(0, levels // 8, tail, jnp.zeros((rows, cells), jnp.float32))
+    lax.fori_loop(0, levels // 16, tail, jnp.zeros((rows, cells), jnp.float32))
     for field in ORDER:
         exchange(field).wait_send()
 

time: 21.1 us -> 21.1 us (level)
  no operation moved by 1% of the time
where the time goes in v7:
time: 21.1 us; the launch traced here: 21 us
  Pallas kernels  21 us (100%)
    pallas_call x1, Pallas kernels, on_pair(): pl.pallas_call(filter_kernel, in_specs=[there] * 11, out_specs=[close] *...  18.2 us
    pallas_call x1, Pallas kernels, on_pair(): pl.pallas_call(final_kernel, in_specs=[scalars] + [close] * 2, out_specs=...  2.79 us

profile of v7, /device:TPU:0, one launch (start us, length us, event | category | flops | bytes accessed | tf_op | source)
XLA Modules:
  0.0 21.0 jit_solution(14221476977213270838)
XLA Ops:
  0.0 0.0 copy-start
  0.0 18.2 %shard_map.109 = (f32[3,32,8,1536]{3,2,1,0:T(8,128)S(1)}, f32[2,2,32,1536]{3,2,1,0:T(8,128)S(1)}) custom-call(f32[64]{0:T(128)} %merid_hbm.1, s32[64]{0:T(128)} %cuts_hbm.1, s32[64]{0:T(128)} %flags_hbm.1, f32[64]{0:T(128)} %zonal_hbm.1, f32[64]{0:T(128)} %coriolis_hbm.1, f32[32]{0:T(128)} %weight_ref.1, f32[3,32,8,1536]{3,2,1,0:T(8,128)} %x_hbm.1, ...), custom_call_target="tpu_custom_call" | custom-call | tf_op jit(solution)/shard_map/pallas_call | solution.py:536
  18.2 0.0 copy-done
  18.2 2.8 %shard_map.110 = f32[3,32,8,1536]{3,2,1,0:T(8,128)} custom-call(f32[32]{0:T(128)S(1)} %copy-done, f32[3,32,8,1536]{3,2,1,0:T(8,128)S(1)} %get-tuple-element.7.part_ref, f32[2,2,32,1536]{3,2,1,0:T(8,128)S(1)} %get-tuple-element.8.edges_ref), custom_call_target="tpu_custom_call" | custom-call | tf_op jit(solution)/shard_map/pallas_call | solution.py:579
Async XLA Ops:
  0.0 18.2 %copy-start = (f32[32]{0:T(128)S(1)}, f32[32]{0:T(128)}, u32[]{:S(2)}) copy-start(f32[32]{0:T(128)} %weight_ref.1) | copy-start | bytes 388
